TPU v7x, 32 devices: a whole 2x2x4 slice. The times are simulated.
32 devices in a mesh: dp: 8 (over z, x), tensor: 4 (over y, core).
Axes of the slice: x: 2, y: 2, z: 4, core: 2. Of those that a mesh axis runs over, the one named last changes fastest.
Arguments:
- tokens: bfloat16 [16384, 1024], P(('dp', 'tensor')), may hold values from -6 to 6
- mixer_gain: float32 [1024], replicated, may hold values from 0.25 to 1.75
- in_weight: bfloat16 [3, 1024, 1024], P(None, None, 'tensor'), may hold values from -0.1875 to 0.1875
- conv_weight: float32 [3, 1024], P(None, 'tensor'), may hold values from -3 to 3
- out_weight: bfloat16 [1024, 1024], P('tensor'), may hold values from -0.1875 to 0.1875
- mlp_gain: float32 [1024], replicated, may hold values from 0.25 to 1.75
- gate_weight: bfloat16 [1024, 4608], P(None, 'tensor'), may hold values from -0.1875 to 0.1875
- up_weight: bfloat16 [1024, 4608], P(None, 'tensor'), may hold values from -0.1875 to 0.1875
- down_weight: bfloat16 [4608, 1024], P('tensor'), may hold values from -0.125 to 0.125
- out_grad: bfloat16 [16384, 1024], P(('dp', 'tensor')), may hold values from -6 to 6
Outputs:
- output: bfloat16 [16384, 1024], P(('dp', 'tensor'))
- input_grad: bfloat16 [16384, 1024], P(('dp', 'tensor'))
- mixer_gain_grad: float32 [1024], replicated
- in_weight_grad: float32 [3, 1024, 1024], P(None, None, 'tensor')
- conv_weight_grad: float32 [3, 1024], P(None, 'tensor')
- out_weight_grad: float32 [1024, 1024], P('tensor')
- mlp_gain_grad: float32 [1024], replicated
- gate_weight_grad: float32 [1024, 4608], P(None, 'tensor')
- up_weight_grad: float32 [1024, 4608], P(None, 'tensor')
- down_weight_grad: float32 [4608, 1024], P('tensor')
All inputs are finite; a program needn't handle non-finite values.
Results may differ from a plain program's by a relative error of at most 0.011.
Values may be sent and summed in bfloat16 or wider, within the bound.
A program may use at most 192 MiB of HBM per device.

v0:
```python
import jax
import jax.numpy as jnp
from jax import lax
from jax.sharding import PartitionSpec as P

LEN = 1024


def rms_scale(values):
    return lax.rsqrt(jnp.mean(values * values, axis=-1, keepdims=True) + 1e-05)


def norm_back(upstream, values, scale, gain_vec):
    scaled = upstream * gain_vec
    inner = jnp.mean(scaled * values, axis=-1, keepdims=True)
    return scale * (scaled - values * scale * scale * inner)


def body(
    tokens,
    mixer_gain,
    in_weight,
    conv_weight,
    out_weight,
    mlp_gain,
    gate_weight,
    up_weight,
    down_weight,
    out_grad,
):
    chans = in_weight.shape[2]
    inputs = tokens.astype(jnp.float32)
    scale_one = rms_scale(inputs)
    first_local = (inputs * scale_one * mixer_gain).astype(jnp.bfloat16)
    first = lax.all_gather(first_local, "tensor", axis=0, tiled=True)
    streams = jnp.einsum("td,kdc->ktc", first, in_weight, preferred_element_type=jnp.float32)
    product = (streams[0] * streams[2]).reshape(-1, LEN, chans)
    padded = jnp.pad(product, ((0, 0), (2, 0), (0, 0)))
    mixed = (
        conv_weight[0] * padded[:, :-2]
        + conv_weight[1] * padded[:, 1:-1]
        + conv_weight[2] * padded[:, 2:]
    )
    mixed_flat = mixed.reshape(-1, chans)
    gated = (streams[1] * mixed_flat).astype(jnp.bfloat16)
    middle = inputs + lax.psum_scatter(
        jnp.dot(gated, out_weight, preferred_element_type=jnp.float32),
        "tensor",
        scatter_dimension=0,
        tiled=True,
    )
    scale_two = rms_scale(middle)
    second_local = (middle * scale_two * mlp_gain).astype(jnp.bfloat16)
    second = lax.all_gather(second_local, "tensor", axis=0, tiled=True)
    gate = jnp.dot(second, gate_weight, preferred_element_type=jnp.float32)
    upper = jnp.dot(second, up_weight, preferred_element_type=jnp.float32)
    sigma = jax.nn.sigmoid(gate)
    activated = gate * sigma
    hidden = (activated * upper).astype(jnp.bfloat16)
    output = (
        middle
        + lax.psum_scatter(
            jnp.dot(hidden, down_weight, preferred_element_type=jnp.float32),
            "tensor",
            scatter_dimension=0,
            tiled=True,
        )
    ).astype(jnp.bfloat16)
    cotangent = lax.all_gather(out_grad, "tensor", axis=0, tiled=True)
    down_grad = jnp.dot(hidden.T, cotangent, preferred_element_type=jnp.float32)
    hidden_grad = jnp.dot(cotangent, down_weight.T, preferred_element_type=jnp.float32)
    gate_grad = (hidden_grad * upper * sigma * (1.0 + gate * (1.0 - sigma))).astype(jnp.bfloat16)
    up_grad = (hidden_grad * activated).astype(jnp.bfloat16)
    gate_w_grad = jnp.dot(second.T, gate_grad, preferred_element_type=jnp.float32)
    up_w_grad = jnp.dot(second.T, up_grad, preferred_element_type=jnp.float32)
    second_grad = lax.psum_scatter(
        jnp.dot(gate_grad, gate_weight.T, preferred_element_type=jnp.float32)
        + jnp.dot(up_grad, up_weight.T, preferred_element_type=jnp.float32),
        "tensor",
        scatter_dimension=0,
        tiled=True,
    )
    mlp_gain_part = jnp.sum(second_grad * middle * scale_two, axis=0)
    middle_grad = out_grad.astype(jnp.float32) + norm_back(second_grad, middle, scale_two, mlp_gain)
    branch_grad = lax.all_gather(middle_grad.astype(jnp.bfloat16), "tensor", axis=0, tiled=True)
    out_w_grad = jnp.dot(gated.T, branch_grad, preferred_element_type=jnp.float32)
    gated_grad = jnp.dot(branch_grad, out_weight.T, preferred_element_type=jnp.float32)
    mixed_grad = (gated_grad * streams[1]).reshape(-1, LEN, chans)
    c_grad = gated_grad * mixed_flat
    trailing = jnp.pad(mixed_grad, ((0, 0), (0, 2), (0, 0)))
    product_grad = (
        conv_weight[2] * trailing[:, :-2]
        + conv_weight[1] * trailing[:, 1:-1]
        + conv_weight[0] * trailing[:, 2:]
    ).reshape(-1, chans)
    conv_grad = jnp.stack(
        [jnp.sum(mixed_grad * padded[:, tap : tap + LEN], axis=(0, 1)) for tap in range(3)]
    )
    stream_grad = jnp.stack([product_grad * streams[2], c_grad, product_grad * streams[0]]).astype(
        jnp.bfloat16
    )
    in_w_grad = jnp.einsum("td,ktc->kdc", first, stream_grad, preferred_element_type=jnp.float32)
    first_grad = lax.psum_scatter(
        jnp.einsum("ktc,kdc->td", stream_grad, in_weight, preferred_element_type=jnp.float32),
        "tensor",
        scatter_dimension=0,
        tiled=True,
    )
    mixer_gain_part = jnp.sum(first_grad * inputs * scale_one, axis=0)
    input_grad = (middle_grad + norm_back(first_grad, inputs, scale_one, mixer_gain)).astype(
        jnp.bfloat16
    )
    (
        in_w_grad,
        conv_grad,
        out_w_grad,
        gate_w_grad,
        up_w_grad,
        down_grad,
        mixer_gain_part,
        mlp_gain_part,
    ) = lax.psum(
        (
            in_w_grad,
            conv_grad,
            out_w_grad,
            gate_w_grad,
            up_w_grad,
            down_grad,
            mixer_gain_part,
            mlp_gain_part,
        ),
        "dp",
    )
    mixer_gain_grad, mlp_gain_grad = lax.psum((mixer_gain_part, mlp_gain_part), "tensor")
    return (
        output,
        input_grad,
        mixer_gain_grad,
        in_w_grad,
        conv_grad,
        out_w_grad,
        mlp_gain_grad,
        gate_w_grad,
        up_w_grad,
        down_grad,
    )


def solution(mesh):
    return jax.shard_map(
        body,
        mesh=mesh,
        in_specs=(
            P(("dp", "tensor"), None),
            P(),
            P(None, None, "tensor"),
            P(None, "tensor"),
            P("tensor", None),
            P(),
            P(None, "tensor"),
            P(None, "tensor"),
            P("tensor", None),
            P(("dp", "tensor"), None),
        ),
        out_specs=(
            P(("dp", "tensor"), None),
            P(("dp", "tensor"), None),
            P(),
            P(None, None, "tensor"),
            P(None, "tensor"),
            P("tensor", None),
            P(),
            P(None, "tensor"),
            P(None, "tensor"),
            P("tensor", None),
        ),
        check_vma=False,
    )
```

profile of v0, /device:TPU:0, one launch (start us, length us, event | category | flops | bytes accessed | tf_op | source)
XLA Modules:
  0.0 1110.8 jit_solution(13589124181223253383)
XLA Ops:
  7.2 1.7 fusion.16
  8.9 2.5 fusion.10
  11.5 37.3 %all-gather.5.cloned.1.call-done = bf16[2048,1024]{1,0:T(8,128)(2,1)} async-done(((bf16[512,1024]{1,0:T(8,128)(2,1)}), bf16[2048,1024]{1,0:T(8,128)(2,1)}) %all-gather.5.cloned.1.call-update) | async-done | bytes 4194320 | tf_op jit(solution)/shard_map/all_gather | solution.py:35
  48.8 5.6 fusion.5
  54.8 0.6 multiply_add_fusion.2
  55.4 1.7 copy-done.1
  57.8 0.7 copy-done.6
  58.5 4.5 fusion.34
  63.2 71.8 %reduce-scatter.5.cloned.1.call-done = f32[512,1024]{1,0:T(8,128)} async-done(((f32[2048,1024]{1,0:T(8,128)}), f32[512,1024]{1,0:T(8,128)}) %reduce-scatter.5.cloned.1.call-update) | async-done | bytes 2097168 | tf_op jit(solution)/shard_map/reduce_scatter | solution.py:46
  135.0 1.9 multiply_reduce_fusion.4
  136.9 1.3 copy-done.2
  138.2 1.2 multiply_convert_fusion.3
  140.6 33.5 %all-gather.7.cloned.1.call-done = bf16[2048,1024]{1,0:T(8,128)(2,1)} async-done(((bf16[512,1024]{1,0:T(8,128)(2,1)}), bf16[2048,1024]{1,0:T(8,128)(2,1)}) %all-gather.7.cloned.1.call-update) | async-done | bytes 4194320 | tf_op jit(solution)/shard_map/all_gather | solution.py:54
  174.1 10.6 fusion.36
  184.7 8.0 fusion.35
  192.6 17.5 %all-gather.9.cloned.1.call-done = bf16[2048,1024]{1,0:T(8,128)(2,1)} async-done(((bf16[512,1024]{1,0:T(8,128)(2,1)}), bf16[2048,1024]{1,0:T(8,128)(2,1)}) %all-gather.9.cloned.1.call-update) | async-done | bytes 4194320 | tf_op jit(solution)/shard_map/all_gather | solution.py:69
  210.1 18.7 %multiply_convert_fusion = (bf16[2048,1152]{1,0:T(8,128)(2,1)}, bf16[2048,1152]{1,0:T(8,128)(2,1)}, bf16[2048,1152]{1,0:T(8,128)(2,1)}) fusion(f32[2048,1152]{1,0:T(8,128)} %fusion.35, f32[2048,1152]{1,0:T(8,128)} %fusion.36, bf16[2048,1024]{1,0:T(8,128)(2,1)} %all-gather.9.cloned.1.call-done, bf16[1152,1024]{1,0:T(8,128)(2,1)S(1)} %copy-done), kind=kOutput, calls=%fused_computation | convolution fusion | flops 4867227648 | bytes 39583744 | tf_op jit(solution)/shard_map/dot_general | solution.py:71
  228.9 7.7 fusion.38
  236.6 8.3 convolution_add_fusion
  245.1 71.6 %reduce-scatter.9.cloned.1.call-done = f32[512,1024]{1,0:T(8,128)} async-done(((f32[2048,1024]{1,0:T(8,128)}), f32[512,1024]{1,0:T(8,128)}) %reduce-scatter.9.cloned.1.call-update) | async-done | bytes 2097168 | tf_op jit(solution)/shard_map/reduce_scatter | solution.py:76
  316.8 2.9 multiply_reduce_fusion
  320.3 2.9 fusion.31
  323.2 34.6 %all-gather.11.cloned.1.call-done = bf16[2048,1024]{1,0:T(8,128)(2,1)} async-done(((bf16[512,1024]{1,0:T(8,128)(2,1)}), bf16[2048,1024]{1,0:T(8,128)(2,1)}) %all-gather.11.cloned.1.call-update) | async-done | bytes 4194320 | tf_op jit(solution)/shard_map/all_gather | solution.py:85
  357.8 6.0 multiply_reduce_fusion.2
  364.2 1.0 copy-done.4
  365.8 2.8 fusion.21
  368.6 0.9 copy-done.18
  369.9 5.8 convolution_bitcast_fusion
  375.7 10.7 fusion.37
  386.7 11.2 %fusion.42 = f32[1152,1024]{1,0:T(8,128)} fusion(bf16[2048,1152]{1,0:T(8,128)(2,1)} %get-tuple-element.41, bf16[2048,1024]{1,0:T(8,128)(2,1)} %all-gather.9.cloned.1.call-done), kind=kOutput, calls=%fused_computation.73 | convolution fusion | flops 4831838208 | bytes 13631488 | tf_op jit(solution)/shard_map/dot_general | solution.py:70
  397.9 10.5 fusion.41
  408.5 7.7 fusion.40
  416.2 2.2 fusion.39
  418.5 1.3 copy-done.27
  419.7 5.2 fusion.26
  425.0 3.3 fusion.20
  428.3 19.2 %reduce-scatter.11.cloned.1.call-done = f32[512,1024]{1,0:T(8,128)} async-done(((f32[2048,1024]{1,0:T(8,128)}), f32[512,1024]{1,0:T(8,128)}) %reduce-scatter.11.cloned.1.call-update) | async-done | bytes 2097168 | tf_op jit(solution)/shard_map/reduce_scatter | solution.py:103
  447.5 2.3 fusion.19
  449.9 37.1 %all-reduce.2 = (f32[1024]{0:T(1024)S(1)}, f32[3,256]{1,0:T(4,128)}, f32[1024]{0:T(1024)S(1)}) all-reduce(f32[1024]{0:T(1024)S(1)} %get-tuple-element.24, f32[3,256]{1,0:T(4,128)S(1)} %pad_maximum_fusion.3, f32[1024]{0:T(1024)S(1)} %get-tuple-element.20), channel_id=1, replica_groups=mesh['dp'=8,'tensor'=4] {'dp'}, use_global_device_ids=true, to_apply=%region_9.10 | all-reduce | flops 2816 | bytes 22528 | tf_op jit(solution)/shard_map/psum | solution.py:122
  486.9 7.1 all-reduce.4
  494.0 28.3 %reduce-scatter.7.cloned.1.call-done = f32[512,1024]{1,0:T(8,128)} async-done(((f32[2048,1024]{1,0:T(8,128)}), f32[512,1024]{1,0:T(8,128)}) %reduce-scatter.7.cloned.1.call-update) | async-done | bytes 2097168 | tf_op jit(solution)/shard_map/reduce_scatter | solution.py:62
  522.3 5.4 fusion.15
  527.7 560.9 %all-reduce.7.cloned.1.call-done = (f32[3,1024,256]{1,2,0:T(8,128)}, f32[256,1024]{1,0:T(8,128)}, f32[1024,1152]{1,0:T(8,128)}, f32[1024,1152]{1,0:T(8,128)}, f32[1152,1024]{1,0:T(8,128)}) async-done(((f32[3,1024,256]{1,2,0:T(8,128)}, f32[256,1024]{1,0:T(8,128)}, f32[1024,1152]{1,0:T(8,128)}, f32[1024,1152]{1,0:T(8,128)}, f32[1152,1024]{1,0:T(8,128)}), (f32[3,1024,256]{1,2,0:T(8,128)}, ...) | async-done | bytes 18350096 | tf_op jit(solution)/shard_map/psum | solution.py:122
  1088.6 3.6 copy.21
  1092.2 1.0 copy.28
  1093.2 5.2 copy.29
  1098.4 2.4 copy.30
  1101.8 2.2 copy.31
  (102 shorter events, 5.9 us)
Async XLA Ops:
  7.2 202.9 %copy-start = (bf16[1152,1024]{1,0:T(8,128)(2,1)S(1)}, bf16[1152,1024]{1,0:T(8,128)(2,1)}, u32[]{:S(2)}) copy-start(bf16[1152,1024]{1,0:T(8,128)(2,1)} %param.18) | copy-start | bytes 7077892
  7.2 4.3 copy-start.26
  7.2 41.6 %all-gather.5.cloned.1.call-start = ((), (), s32[]{:S(2)}) async-start(), calls=%async_computation.4 | async-start | bytes 5242880 | tf_op jit(solution)/shard_map/all_gather | solution.py:35
  8.9 45.5 %copy-start.24 = (f32[512]{0:T(512)}, f32[512]{0:T(512)S(1)}, u32[]{:S(2)}) copy-start(f32[512]{0:T(512)S(1)} %add_rsqrt_fusion.1) | copy-start | bytes 6148
  11.5 123.5 %reduce-scatter.5.cloned.1.call-start = ((), (), s32[]{:S(2)}) async-start(), calls=%async_computation.5 | async-start | bytes 10485760 | tf_op jit(solution)/shard_map/reduce_scatter | solution.py:46
  54.5 2.6 copy-start.1
  54.7 3.1 copy-start.9
  57.1 1.4 copy-start.6
  57.1 1.4 copy-start.14
  58.5 4.5 copy-start.11
  63.1 71.9 %copy-start.5 = (bf16[512,1024]{1,0:T(8,128)(2,1)S(1)}, bf16[512,1024]{1,0:T(8,128)(2,1)}, u32[]{:S(2)}) copy-start(bf16[512,1024]{1,0:T(8,128)(2,1)} %param.10) | copy-start | bytes 3145732
  63.1 75.1 %copy-start.22 = (f32[1024]{0:T(1024)S(1)}, f32[1024]{0:T(1024)}, u32[]{:S(2)}) copy-start(f32[1024]{0:T(1024)} %param.15) | copy-start | bytes 12292
  63.1 111.0 %all-gather.7.cloned.1.call-start = ((), (), s32[]{:S(2)}) async-start(), calls=%async_computation.6 | async-start | bytes 5242880 | tf_op jit(solution)/shard_map/all_gather | solution.py:54
  136.9 1.3 copy-start.2
  139.5 70.6 %all-gather.9.cloned.1.call-start = ((), (), s32[]{:S(2)}) async-start(), calls=%async_computation.8 | async-start | bytes 5242880 | tf_op jit(solution)/shard_map/all_gather | solution.py:69
  140.0 176.7 %reduce-scatter.9.cloned.1.call-start = ((), (), s32[]{:S(2)}) async-start(), calls=%async_computation.9 | async-start | bytes 10485760 | tf_op jit(solution)/shard_map/reduce_scatter | solution.py:76
  174.1 10.6 copy-start.28
  174.1 10.6 copy-start.30
  210.1 18.7 %copy-start.31 = (bf16[1024,1152]{1,0:T(8,128)(2,1)S(1)}, bf16[1024,1152]{1,0:T(8,128)(2,1)}, u32[]{:S(2)}) copy-start(bf16[1024,1152]{1,0:T(8,128)(2,1)} %param.16) | copy-start | bytes 7077892
  228.9 7.7 copy-start.32
  228.9 7.7 copy-start.34
  244.9 112.9 %all-gather.11.cloned.1.call-start = ((), (), s32[]{:S(2)}) async-start(), calls=%async_computation.10 | async-start | bytes 5242880 | tf_op jit(solution)/shard_map/all_gather | solution.py:85
  316.8 2.9 copy-start.3
  316.8 3.5 copy-start.8
  323.2 124.3 %reduce-scatter.11.cloned.1.call-start = ((), (), s32[]{:S(2)}) async-start(), calls=%async_computation.11 | async-start | bytes 10485760 | tf_op jit(solution)/shard_map/reduce_scatter | solution.py:103
  357.8 6.0 copy-start.7
  363.8 1.3 copy-start.4
  364.1 4.4 copy-start.15
  365.7 4.1 copy-start.33
  368.6 1.0 copy-start.18
  368.6 1.3 copy-start.20
  375.7 146.7 %reduce-scatter.7.cloned.1.call-start = ((), (), s32[]{:S(2)}) async-start(), calls=%async_computation.7 | async-start | bytes 10485760 | tf_op jit(solution)/shard_map/reduce_scatter | solution.py:62
  386.4 702.2 %all-reduce.7.cloned.1.call-start = ((), (), s32[]{:S(2)}) async-start(), calls=%async_computation.12 | async-start | bytes 36700160 | tf_op jit(solution)/shard_map/psum | solution.py:122
  386.7 11.3 %copy-start.29 = (bf16[2048,1024]{1,0:T(8,128)(2,1)S(1)}, bf16[2048,1024]{1,0:T(8,128)(2,1)}, u32[]{:S(2)}) copy-start(bf16[2048,1024]{1,0:T(8,128)(2,1)} %all-gather.7.cloned.1.call-done) | copy-start | bytes 12582916
  386.7 21.8 %slice-start.2 = ((s8[4718592]{0:T(1024)(128)(4,1)}), s8[4194304]{0:T(1024)(128)(4,1)S(1)}, s32[]{:S(2)}) async-start(s8[4718592]{0:T(1024)(128)(4,1)} %bitcast.95), calls=%async_computation.15 | async-start | bytes 8388608
  397.9 10.5 slice-start.3
  408.4 7.7 copy-start.10
  408.4 7.7 copy-start.12
  416.2 2.3 copy-start.16
  416.2 2.3 copy-start.19
  416.2 2.3 copy-start.21
  416.2 3.5 copy-start.27
  425.0 22.6 %copy-start.23 = (f32[1024]{0:T(1024)S(1)}, f32[1024]{0:T(1024)}, u32[]{:S(2)}) copy-start(f32[1024]{0:T(1024)} %param.11) | copy-start | bytes 12292
  425.0 22.6 %copy-start.25 = (f32[512]{0:T(512)S(1)}, f32[512]{0:T(512)}, u32[]{:S(2)}) copy-start(f32[512]{0:T(512)} %copy-done.24) | copy-start | bytes 6148
  1088.6 3.6 copy-start.17
  1093.2 5.2 copy-start.13
  1093.2 8.0 slice-start
  1098.4 3.4 slice-start.1
Sparse Core Ops, SparseCore 0:
  11.6 37.1 all-gather.4
  63.2 71.7 reduce-scatter.4
  139.6 34.4 all-gather.6
  175.6 34.4 all-gather.8
  245.0 71.6 reduce-scatter.8
  323.3 34.4 all-gather.10
  375.8 71.7 reduce-scatter.10
  450.3 71.9 reduce-scatter.6
  528.7 559.8 all-reduce.6
where the time goes:
time: 1120 us; the launch traced here: 1110 us
  waiting for transfers between devices  875 us (78%)
  matrix products  123 us (11%)
  blocking collectives  44.1 us (4%)
  other arithmetic  29.1 us (3%)
  local copies, waits for them, and re-layouts  23.7 us (2%)
  between operations  14.5 us (1%)
    psum x1, waiting for transfers between devices, body(): lax.psum((in_w_grad, conv_grad, out_w_grad, gate_w_grad, up_w_grad, down_...  561 us
    reduce_scatter x1, waiting for transfers between devices, body(): lax.psum_scatter(jnp.dot(gated, out_weight, preferred_element_type=jnp.fl...  71.8 us
    reduce_scatter x1, waiting for transfers between devices, body(): lax.psum_scatter(jnp.dot(gate_grad, gate_weight.T, preferred_element_type...  71.6 us
    all_gather x1, waiting for transfers between devices, body(): first = lax.all_gather(first_local, 'tensor', axis=0, tiled=True)  37.3 us
    psum x1, blocking collectives, body(): lax.psum((in_w_grad, conv_grad, out_w_grad, gate_w_grad, up_w_grad, down_...  37.1 us
    all_gather x1, waiting for transfers between devices, body(): lax.all_gather(middle_grad.astype(jnp.bfloat16), 'tensor', axis=0, tiled=...  34.6 us
    all_gather x1, waiting for transfers between devices, body(): second = lax.all_gather(second_local, 'tensor', axis=0, tiled=True)  33.5 us
    reduce_scatter x1, waiting for transfers between devices, body(): lax.psum_scatter(jnp.dot(hidden, down_weight, preferred_element_type=jnp....  28.3 us
  transfers between devices with their start and end apart: 9, of which 9 were waited for; matrix products, arithmetic and copies ran while one was open for 7% of the time, Pallas kernels for 0%

commit v1 on v0

v1 whole, which is shorter than its diff:
```python
import functools

import jax
import jax.numpy as jnp
from jax import lax
from jax.sharding import PartitionSpec as P

LEN = 1024
F32 = jnp.float32
BF16 = jnp.bfloat16


def rms_scale(values):
    return lax.rsqrt(jnp.mean(values * values, axis=-1, keepdims=True) + 1e-05)


def norm_back(upstream, values, scale, gain_vec):
    scaled = upstream * gain_vec
    inner = jnp.mean(scaled * values, axis=-1, keepdims=True)
    return scale * (scaled - values * scale * scale * inner)


def dot(a, b):
    return jnp.dot(a, b, preferred_element_type=F32)


def dot_rows(a, b):
    return lax.dot_general(a, b, (((0,), (0,)), ((), ())), preferred_element_type=F32)


def dot_cols(a, b):
    return lax.dot_general(a, b, (((1,), (1,)), ((), ())), preferred_element_type=F32)


def body(
    size,
    tokens,
    mixer_gain,
    in_weight,
    conv_weight,
    out_weight,
    mlp_gain,
    gate_weight,
    up_weight,
    down_weight,
    out_grad,
):
    n_dp, n_tensor = size["dp"], size["tensor"]
    chans = in_weight.shape[2]
    dp_at = lax.axis_index("dp")
    core = lax.rem(lax.axis_index("tensor"), 2)

    def swap(value, axis, bit):
        return lax.ppermute(value, axis, [(i, i ^ bit) for i in range(size[axis])])

    def ordered(side, own, other):
        return jnp.where(side == 0, jnp.concatenate([own, other]), jnp.concatenate([other, own]))

    def parted(side, value):
        two = value.reshape(2, value.shape[0] // 2, *value.shape[1:])
        keep = lax.dynamic_index_in_dim(two, side, 0, keepdims=False)
        give = lax.dynamic_index_in_dim(two, 1 - side, 0, keepdims=False)
        return keep, give

    def gather(own):
        far = swap(own, "tensor", 2)
        near = swap(own, "tensor", 1)
        far_near = swap(far, "tensor", 1)
        return ordered(core, own, near), ordered(core, far, far_near)

    def scatter(mine, other):
        keep, give = parted(core, other)
        total = keep + swap(give.astype(BF16), "tensor", 1).astype(F32)
        got_far = swap(total.astype(BF16), "tensor", 2)
        keep, give = parted(core, mine)
        return keep + swap(give.astype(BF16), "tensor", 1).astype(F32) + got_far.astype(F32)

    dp_bits = [1 << k for k in range(n_dp.bit_length() - 1)]

    def sum_dp(value, turn):
        bits = dp_bits[turn:] + dp_bits[:turn]
        current = value
        for bit in bits:
            keep, give = parted((dp_at // bit) % 2, current)
            current = keep + swap(give.astype(BF16), "dp", bit).astype(F32)
        current = current.astype(BF16)
        for bit in reversed(bits):
            current = ordered((dp_at // bit) % 2, current, swap(current, "dp", bit))
        return current.astype(F32)

    def sum_dp_split(value):
        half = value.shape[0] // 2
        return jnp.concatenate([sum_dp(value[:half], 0), sum_dp(value[half:], 1)])

    def sum_small(value, axis):
        bit = 1
        while bit < size[axis]:
            value = value + swap(value, axis, bit)
            bit *= 2
        return value

    in_flat = jnp.concatenate([in_weight[0], in_weight[1], in_weight[2]], axis=1)

    def conv_forward(first):
        streams = dot(first, in_flat)
        b, c, x = streams[:, :chans], streams[:, chans : 2 * chans], streams[:, 2 * chans :]
        product = (b * x).reshape(-1, LEN, chans)
        padded = jnp.pad(product, ((0, 0), (2, 0), (0, 0)))
        mixed = (
            conv_weight[0] * padded[:, :-2]
            + conv_weight[1] * padded[:, 1:-1]
            + conv_weight[2] * padded[:, 2:]
        ).reshape(-1, chans)
        gated = (c * mixed).astype(BF16)
        return (b, c, x, padded, mixed, gated), dot(gated, out_weight)

    def conv_backward(kept, branch_grad):
        b, c, x, padded, mixed, gated = kept
        gated_grad = dot_cols(branch_grad, out_weight)
        mixed_grad = (gated_grad * c).reshape(-1, LEN, chans)
        c_grad = gated_grad * mixed
        trailing = jnp.pad(mixed_grad, ((0, 0), (0, 2), (0, 0)))
        product_grad = (
            conv_weight[2] * trailing[:, :-2]
            + conv_weight[1] * trailing[:, 1:-1]
            + conv_weight[0] * trailing[:, 2:]
        ).reshape(-1, chans)
        conv_grad = jnp.stack(
            [jnp.sum(mixed_grad * padded[:, tap : tap + LEN], axis=(0, 1)) for tap in range(3)]
        )
        stream_grad = jnp.concatenate(
            [product_grad * x, c_grad, product_grad * b], axis=1
        ).astype(BF16)
        return stream_grad, conv_grad, dot_cols(stream_grad, in_flat)

    def mlp_forward(second):
        gate = dot(second, gate_weight)
        upper = dot(second, up_weight)
        hidden = (gate * jax.nn.sigmoid(gate) * upper).astype(BF16)
        return gate, upper, hidden

    def mlp_backward(gate, upper, cotangent):
        hidden_grad = dot_cols(cotangent, down_weight)
        sigma = jax.nn.sigmoid(gate)
        gate_grad = (hidden_grad * upper * sigma * (1.0 + gate * (1.0 - sigma))).astype(BF16)
        up_grad = (hidden_grad * gate * sigma).astype(BF16)
        return gate_grad, up_grad, dot_cols(gate_grad, gate_weight) + dot_cols(up_grad, up_weight)

    inputs = tokens.astype(F32)
    scale_one = rms_scale(inputs)
    first_m, first_o = gather((inputs * scale_one * mixer_gain).astype(BF16))
    kept_o, part_o = conv_forward(first_o)
    kept_m, part_m = conv_forward(first_m)
    middle = inputs + scatter(part_m, part_o)
    scale_two = rms_scale(middle)
    second_m, second_o = gather((middle * scale_two * mlp_gain).astype(BF16))
    cot_m, cot_o = gather(out_grad)
    gate_m, upper_m, hidden_m = mlp_forward(second_m)
    gate_o, upper_o, hidden_o = mlp_forward(second_o)
    down_grad = sum_dp_split(dot_rows(hidden_m, cot_m) + dot_rows(hidden_o, cot_o))
    output = (middle + scatter(dot(hidden_m, down_weight), dot(hidden_o, down_weight))).astype(BF16)

    gate_grad_o, up_grad_o, back_o = mlp_backward(gate_o, upper_o, cot_o)
    gate_grad_m, up_grad_m, back_m = mlp_backward(gate_m, upper_m, cot_m)
    second_grad = scatter(back_m, back_o)
    gate_w_grad = sum_dp_split(dot_rows(second_m, gate_grad_m) + dot_rows(second_o, gate_grad_o))
    up_w_grad = sum_dp_split(dot_rows(second_m, up_grad_m) + dot_rows(second_o, up_grad_o))

    mlp_gain_part = jnp.sum(second_grad * middle * scale_two, axis=0)
    middle_grad = out_grad.astype(F32) + norm_back(second_grad, middle, scale_two, mlp_gain)
    branch_m, branch_o = gather(middle_grad.astype(BF16))
    out_w_grad = sum_dp(dot_rows(kept_m[5], branch_m) + dot_rows(kept_o[5], branch_o), 1)
    stream_grad_o, conv_grad_o, back_o = conv_backward(kept_o, branch_o)
    stream_grad_m, conv_grad_m, back_m = conv_backward(kept_m, branch_m)
    in_flat_grad = dot_rows(first_m, stream_grad_m) + dot_rows(first_o, stream_grad_o)
    in_w_grad = jnp.stack(
        [sum_dp(in_flat_grad[:, k * chans : (k + 1) * chans], k % 2) for k in range(3)]
    )
    first_grad = scatter(back_m, back_o)
    mixer_gain_part = jnp.sum(first_grad * inputs * scale_one, axis=0)
    input_grad = (middle_grad + norm_back(first_grad, inputs, scale_one, mixer_gain)).astype(BF16)

    conv_grad = sum_small(conv_grad_m + conv_grad_o, "dp")
    gains = sum_small(sum_small(jnp.stack([mixer_gain_part, mlp_gain_part]), "tensor"), "dp")
    return (
        output,
        input_grad,
        gains[0],
        in_w_grad,
        conv_grad,
        out_w_grad,
        gains[1],
        gate_w_grad,
        up_w_grad,
        down_grad,
    )


def solution(mesh):
    size = {"dp": mesh.shape["dp"], "tensor": mesh.shape["tensor"]}
    return jax.shard_map(
        functools.partial(body, size),
        mesh=mesh,
        in_specs=(
            P(("dp", "tensor"), None),
            P(),
            P(None, None, "tensor"),
            P(None, "tensor"),
            P("tensor", None),
            P(),
            P(None, "tensor"),
            P(None, "tensor"),
            P("tensor", None),
            P(("dp", "tensor"), None),
        ),
        out_specs=(
            P(("dp", "tensor"), None),
            P(("dp", "tensor"), None),
            P(),
            P(None, None, "tensor"),
            P(None, "tensor"),
            P("tensor", None),
            P(),
            P(None, "tensor"),
            P(None, "tensor"),
            P("tensor", None),
        ),
        check_vma=False,
    )
```

time: 1120 us -> 584 us (0.52)
  waiting for transfers between devices: 875 us -> 294 us
  starting transfers between devices: 1.28 us -> 89.8 us
  blocking collectives: 44.1 us -> 0 us
  between operations: 14.5 us -> 2.62 us
    psum x1 -> x0, waiting for transfers between devices: 561 us -> none  [body(): lax.psum((in_w_grad, conv_grad, out_w_grad, gate_w_grad, up_w_grad, down_...]
    ppermute x0 -> x92, waiting for transfers between devices: none -> 294 us  [swap(): return lax.ppermute(value, axis, [(i, i ^ bit) for i in range(size[axis])])]
    reduce_scatter x4 -> x0, waiting for transfers between devices: 191 us -> none  [the longest x1 71.8 us: body(): lax.psum_scatter(jnp.dot(gated, out_weight, preferred_element_type=jnp.fl...]
    all_gather x4 -> x0, waiting for transfers between devices: 123 us -> none  [the longest x1 37.3 us: body(): first = lax.all_gather(first_local, 'tensor', axis=0, tiled=True)]
    ppermute x0 -> x92, starting transfers between devices: none -> 89.8 us  [swap(): return lax.ppermute(value, axis, [(i, i ^ bit) for i in range(size[axis])])]
    psum x2 -> x0, blocking collectives: 44.1 us -> none  [the longest x1 37.1 us: body(): lax.psum((in_w_grad, conv_grad, out_w_grad, gate_w_grad, up_w_grad, down_...]
    unnamed x83 -> x126, local copies, waits for them, and re-layouts: 23.7 us -> 9.21 us
    dot_general x15 -> x30, matrix products: 123 us -> 128 us  [the longest x10 48.6 us: dot_rows(): lax.dot_general(a, b, (((0,), (0,)), ((), ())), preferred_element_type=F32)]
  transfers between devices with their start and end apart: 9 -> 92, of which waited for: 9 -> 51; matrix products, arithmetic and copies ran while one was open for 7% -> 28% of each run, Pallas kernels for 0% -> 0%
where the time goes in v1:
time: 584 us; the launch traced here: 575 us
  waiting for transfers between devices  294 us (50%)
  matrix products  128 us (22%)
  starting transfers between devices  89.8 us (15%)
  other arithmetic  39.9 us (7%)
  local copies, waits for them, and re-layouts  20.8 us (4%)
    ppermute x92, waiting for transfers between devices, swap(): return lax.ppermute(value, axis, [(i, i ^ bit) for i in range(size[axis])])  294 us
    ppermute x92, starting transfers between devices, swap(): return lax.ppermute(value, axis, [(i, i ^ bit) for i in range(size[axis])])  89.8 us
    dot_general x10, matrix products, dot_rows(): lax.dot_general(a, b, (((0,), (0,)), ((), ())), preferred_element_type=F32)  48.6 us
    dot_general x10, matrix products, dot(): return jnp.dot(a, b, preferred_element_type=F32)  41.4 us
    dot_general x10, matrix products, dot_cols(): lax.dot_general(a, b, (((1,), (1,)), ((), ())), preferred_element_type=F32)  37.6 us
  transfers between devices with their start and end apart: 92, of which 51 were waited for; matrix products, arithmetic and copies ran while one was open for 28% of the time, Pallas kernels for 0%

profile of v1, /device:TPU:0, one launch (start us, length us, event | category | flops | bytes accessed | tf_op | source)
XLA Modules:
  0.0 574.6 jit_solution(15517813122074569639)
XLA Ops:
  6.9 23.3 %collective-permute-done.2 = bf16[512,1024]{1,0:T(8,128)(2,1)} collective-permute-done((bf16[512,1024]{1,0:T(8,128)(2,1)S(1)}, bf16[512,1024]{1,0:T(8,128)(2,1)}, u32[]{:S(2)}, u32[]{:S(2)}) %collective-permute-start.2) | collective-permute-done | bytes 1048608 | tf_op jit(solution)/shard_map/ppermute | solution.py:54
  31.8 3.9 fusion.54
  35.9 5.3 fusion.53
  54.7 23.9 %collective-permute-done.5 = bf16[512,1024]{1,0:T(8,128)(2,1)S(1)} collective-permute-done((bf16[512,1024]{1,0:T(8,128)(2,1)S(1)}, bf16[512,1024]{1,0:T(8,128)(2,1)S(1)}, u32[]{:S(2)}, u32[]{:S(2)}) %collective-permute-start.5) | collective-permute-done | bytes 1048608 | tf_op jit(solution)/shard_map/ppermute | solution.py:54
  82.4 18.3 %collective-permute-done.14 = bf16[512,1024]{1,0:T(8,128)(2,1)} collective-permute-done((bf16[512,1024]{1,0:T(8,128)(2,1)S(1)}, bf16[512,1024]{1,0:T(8,128)(2,1)}, u32[]{:S(2)}, u32[]{:S(2)}) %collective-permute-start.14) | collective-permute-done | bytes 1048608 | tf_op jit(solution)/shard_map/ppermute | solution.py:54
  102.4 5.8 %fusion.115 = f32[1024,1152]{1,0:T(8,128)S(1)} fusion(bf16[1024,1152]{1,0:T(8,128)(2,1)} %param.16, bf16[512,1024]{1,0:T(8,128)(2,1)} %collective-permute-done.6, bf16[512,1024]{1,0:T(8,128)(2,1)} %multiply_convert_fusion.6, pred[]{:T(512)S(6)} %eq.107), kind=kOutput, calls=%fused_computation.296 | convolution fusion | flops 2425356288 | bytes 9175041 | tf_op jit(solution)/shard_map/dot_general | solution.py:24
  108.3 7.7 %fusion.114 = f32[1024,1152]{1,0:T(8,128)} fusion(bf16[1024,1152]{1,0:T(8,128)(2,1)S(1)} %copy-done.48, bf16[512,1024]{1,0:T(8,128)(2,1)} %collective-permute-done.6, bf16[512,1024]{1,0:T(8,128)(2,1)} %multiply_convert_fusion.6, pred[]{:T(512)S(6)} %eq.107), kind=kOutput, calls=%fused_computation.295 | convolution fusion | flops 2425356288 | bytes 9175041 | tf_op jit(solution)/shard_map/dot_general | solution.py:24
  116.0 9.6 %multiply_convert_fusion.2 = (bf16[1024,1152]{1,0:T(8,128)(2,1)}, bf16[1024,1152]{1,0:T(8,128)(2,1)S(1)}, bf16[1024,1152]{1,0:T(8,128)(2,1)}) fusion(f32[1024,1152]{1,0:T(8,128)S(1)} %fusion.115, f32[1024,1152]{1,0:T(8,128)} %fusion.114, bf16[1152,1024]{1,0:T(8,128)(2,1)S(1)} %copy-done, bf16[512,1024]{1,0:T(8,128)(2,1)} %collective-permute-done.12, ...), kind=kOutput, calls=%fused_computation.2 | convolution fusion | flops 2444230656 | bytes 20971520 | tf_op jit(solution)/shard_map/dot_general | solution.py:32
  138.9 7.5 %fusion.113 = f32[1024,1152]{1,0:T(8,128)} fusion(bf16[1024,1152]{1,0:T(8,128)(2,1)S(1)} %copy-done.61, bf16[512,1024]{1,0:T(8,128)(2,1)} %collective-permute-done.6, bf16[512,1024]{1,0:T(8,128)(2,1)} %multiply_convert_fusion.6, pred[]{:T(512)S(6)} %eq.107), kind=kOutput, calls=%fused_computation.294 | convolution fusion | flops 2425356288 | bytes 9175041 | tf_op jit(solution)/shard_map/dot_general | solution.py:28
  146.7 7.5 %fusion.112 = f32[1024,1152]{1,0:T(8,128)} fusion(bf16[1024,1152]{1,0:T(8,128)(2,1)S(1)} %copy-done.59, bf16[512,1024]{1,0:T(8,128)(2,1)} %collective-permute-done.6, bf16[512,1024]{1,0:T(8,128)(2,1)} %multiply_convert_fusion.6, pred[]{:T(512)S(6)} %eq.107), kind=kOutput, calls=%fused_computation.293 | convolution fusion | flops 2425356288 | bytes 9175041 | tf_op jit(solution)/shard_map/dot_general | solution.py:28
  154.2 6.6 %fusion.51 = f32[1152,1024]{1,0:T(8,128)} fusion(bf16[1024,1152]{1,0:T(8,128)(2,1)S(1)} %copy-done.62, bf16[512,1024]{1,0:T(8,128)(2,1)} %collective-permute-done.12, bf16[512,1024]{1,0:T(8,128)(2,1)S(1)} %copy-done.12, pred[]{:T(512)S(6)} %eq.107), kind=kOutput, calls=%fused_computation.184 | convolution fusion | flops 2425356288 | bytes 9175041 | tf_op jit(solution)/shard_map/dot_general | solution.py:28
  160.8 5.8 %fusion.111 = f32[1024,1152]{1,0:T(8,128)} fusion(bf16[1024,1152]{1,0:T(8,128)(2,1)S(1)} %copy-done.47, bf16[512,1024]{1,0:T(8,128)(2,1)S(1)} %collective-permute-done.9, bf16[512,1024]{1,0:T(8,128)(2,1)S(1)} %collective-permute-done.8, pred[]{:T(512)S(6)} %eq.107), kind=kOutput, calls=%fused_computation.292 | convolution fusion | flops 2425356288 | bytes 9175041 | tf_op jit(solution)/shard_map/dot_general | solution.py:24
  166.5 5.7 fusion.110
  172.3 10.7 %multiply_convert_fusion = (bf16[1024,1152]{1,0:T(8,128)(2,1)}, bf16[1024,1152]{1,0:T(8,128)(2,1)S(1)}, bf16[1024,1152]{1,0:T(8,128)(2,1)}) fusion(f32[1024,1152]{1,0:T(8,128)} %fusion.111, f32[1024,1152]{1,0:T(8,128)} %fusion.110, bf16[1152,1024]{1,0:T(8,128)(2,1)S(1)} %copy-done, bf16[512,1024]{1,0:T(8,128)(2,1)S(1)} %collective-permute-done.15, ...), kind=kOutput, calls=%fused_computation | convolution fusion | flops 2444230656 | bytes 20971520 | tf_op jit(solution)/shard_map/dot_general | solution.py:32
  193.7 5.0 convolution_add_fusion.2
  201.4 6.1 %convolution_add_fusion.1 = f32[1024,1152]{1,0:T(8,128)S(1)} fusion(f32[1024,1152]{1,0:T(8,128)} %fusion.112, bf16[1024,1152]{1,0:T(8,128)(2,1)} %get-tuple-element.35, bf16[512,1024]{1,0:T(8,128)(2,1)S(1)} %copy-done.54, bf16[512,1024]{1,0:T(8,128)(2,1)S(1)} %copy-done.52, pred[]{:T(512)S(6)} %eq.107), kind=kOutput, calls=%fused_computation.9 | convolution fusion | flops 2426535936 | bytes 13893633 | tf_op jit(solution)/shard_map/dot_general | solution.py:28
  209.2 5.9 %convolution_add_fusion = f32[1152,1024]{1,0:T(8,128)S(1)} fusion(f32[1152,1024]{1,0:T(8,128)} %fusion.51, bf16[1024,1152]{1,0:T(8,128)(2,1)S(1)} %copy-done.55, bf16[512,1024]{1,0:T(8,128)(2,1)S(1)} %copy-done.50, bf16[512,1024]{1,0:T(8,128)(2,1)} %collective-permute-done.14, pred[]{:T(512)S(6)} %eq.107), kind=kOutput, calls=%fused_computation.8 | convolution fusion | flops 2426535936 | bytes 13893633 | tf_op jit(solution)/shard_map/dot_general | solution.py:28
  219.0 9.3 %collective-permute-done.74 = bf16[256,1152]{1,0:T(8,128)(2,1)} collective-permute-done((bf16[256,1152]{1,0:T(8,128)(2,1)}, bf16[256,1152]{1,0:T(8,128)(2,1)}, u32[]{:S(2)}, u32[]{:S(2)}) %collective-permute-start.74) | collective-permute-done | bytes 589856 | tf_op jit(solution)/shard_map/ppermute | solution.py:54
  233.6 11.9 %collective-permute-done.86 = bf16[288,1024]{1,0:T(8,128)(2,1)S(1)} collective-permute-done((bf16[288,1024]{1,0:T(8,128)(2,1)S(1)}, bf16[288,1024]{1,0:T(8,128)(2,1)S(1)}, u32[]{:S(2)}, u32[]{:S(2)}) %collective-permute-start.86) | collective-permute-done | bytes 589856 | tf_op jit(solution)/shard_map/ppermute | solution.py:54
  249.4 8.9 %collective-permute-done.80 = bf16[288,1024]{1,0:T(8,128)(2,1)S(1)} collective-permute-done((bf16[288,1024]{1,0:T(8,128)(2,1)S(1)}, bf16[288,1024]{1,0:T(8,128)(2,1)S(1)}, u32[]{:S(2)}, u32[]{:S(2)}) %collective-permute-start.80) | collective-permute-done | bytes 589856 | tf_op jit(solution)/shard_map/ppermute | solution.py:54
  260.2 5.7 collective-permute-done.57
  270.2 9.8 %collective-permute-done.75 = bf16[128,1152]{1,0:T(8,128)(2,1)S(1)} collective-permute-done((bf16[128,1152]{1,0:T(8,128)(2,1)S(1)}, bf16[128,1152]{1,0:T(8,128)(2,1)S(1)}, u32[]{:S(2)}, u32[]{:S(2)}) %collective-permute-start.75) | collective-permute-done | bytes 294944 | tf_op jit(solution)/shard_map/ppermute | solution.py:54
  283.2 11.9 %collective-permute-done.87 = bf16[144,1024]{1,0:T(8,128)(2,1)S(1)} collective-permute-done((bf16[144,1024]{1,0:T(8,128)(2,1)S(1)}, bf16[144,1024]{1,0:T(8,128)(2,1)S(1)}, u32[]{:S(2)}, u32[]{:S(2)}) %collective-permute-start.87) | collective-permute-done | bytes 294944 | tf_op jit(solution)/shard_map/ppermute | solution.py:54
  295.1 3.2 collective-permute-start.64
  308.7 3.8 collective-permute-done.88
  315.1 7.0 %collective-permute-done.82 = bf16[72,1024]{1,0:T(8,128)(2,1)S(1)} collective-permute-done((bf16[72,1024]{1,0:T(8,128)(2,1)S(1)}, bf16[72,1024]{1,0:T(8,128)(2,1)S(1)}, u32[]{:S(2)}, u32[]{:S(2)}) %collective-permute-start.82) | collective-permute-done | bytes 147488 | tf_op jit(solution)/shard_map/ppermute | solution.py:54
  332.4 4.7 collective-permute-done.59
  337.2 9.4 %collective-permute-done.71 = bf16[64,1152]{1,0:T(8,128)(2,1)S(1)} collective-permute-done((bf16[64,1152]{1,0:T(8,128)(2,1)S(1)}, bf16[64,1152]{1,0:T(8,128)(2,1)S(1)}, u32[]{:S(2)}, u32[]{:S(2)}) %collective-permute-start.71) | collective-permute-done | bytes 147488 | tf_op jit(solution)/shard_map/ppermute | solution.py:54
  346.7 3.1 collective-permute-start.78
  350.0 11.6 %collective-permute-done.66 = bf16[128,1152]{1,0:T(8,128)(2,1)S(1)} collective-permute-done((bf16[128,1152]{1,0:T(8,128)(2,1)S(1)}, bf16[128,1152]{1,0:T(8,128)(2,1)S(1)}, u32[]{:S(2)}, u32[]{:S(2)}) %collective-permute-start.66) | collective-permute-done | bytes 294944 | tf_op jit(solution)/shard_map/ppermute | solution.py:54
  361.7 13.4 %collective-permute-done.78 = bf16[128,1152]{1,0:T(8,128)(2,1)S(1)} collective-permute-done((bf16[128,1152]{1,0:T(8,128)(2,1)S(1)}, bf16[128,1152]{1,0:T(8,128)(2,1)S(1)}, u32[]{:S(2)}, u32[]{:S(2)}) %collective-permute-start.78) | collective-permute-done | bytes 294944 | tf_op jit(solution)/shard_map/ppermute | solution.py:54
  382.5 5.1 collective-permute-done.84
  387.8 12.5 %collective-permute-done.67 = bf16[256,1152]{1,0:T(8,128)(2,1)S(1)} collective-permute-done((bf16[256,1152]{1,0:T(8,128)(2,1)S(1)}, bf16[256,1152]{1,0:T(8,128)(2,1)S(1)}, u32[]{:S(2)}, u32[]{:S(2)}) %collective-permute-start.67) | collective-permute-done | bytes 589856 | tf_op jit(solution)/shard_map/ppermute | solution.py:54
  402.8 10.1 %collective-permute-done.79 = bf16[256,1152]{1,0:T(8,128)(2,1)S(1)} collective-permute-done((bf16[256,1152]{1,0:T(8,128)(2,1)S(1)}, bf16[256,1152]{1,0:T(8,128)(2,1)S(1)}, u32[]{:S(2)}, u32[]{:S(2)}) %collective-permute-start.79) | collective-permute-done | bytes 589856 | tf_op jit(solution)/shard_map/ppermute | solution.py:54
  421.3 4.2 collective-permute-done.91
  434.1 11.7 %collective-permute-done.20 = bf16[512,1024]{1,0:T(8,128)(2,1)S(1)} collective-permute-done((bf16[512,1024]{1,0:T(8,128)(2,1)S(1)}, bf16[512,1024]{1,0:T(8,128)(2,1)S(1)}, u32[]{:S(2)}, u32[]{:S(2)}) %collective-permute-start.20) | collective-permute-done | bytes 1048608 | tf_op jit(solution)/shard_map/ppermute | solution.py:54
  458.7 3.9 fusion.41
  462.6 4.6 convolution_add_fusion.5
  470.6 5.8 %collective-permute-done.47 = f32[3,256]{1,0:T(4,128)S(1)} collective-permute-done((f32[3,256]{1,0:T(4,128)S(1)}, f32[3,256]{1,0:T(4,128)S(1)}, u32[]{:S(2)}, u32[]{:S(2)}) %collective-permute-start.47) | collective-permute-done | bytes 3104 | tf_op jit(solution)/shard_map/ppermute | solution.py:54
  476.5 3.5 collective-permute-done.48
  481.2 3.4 collective-permute-done.49
  492.1 6.7 %collective-permute-done.50 = bf16[128,1024]{1,0:T(8,128)(2,1)S(1)} collective-permute-done((bf16[128,1024]{1,0:T(8,128)(2,1)S(1)}, bf16[128,1024]{1,0:T(8,128)(2,1)S(1)}, u32[]{:S(2)}, u32[]{:S(2)}) %collective-permute-start.50) | collective-permute-done | bytes 262176 | tf_op jit(solution)/shard_map/ppermute | solution.py:54
  506.0 4.9 collective-permute-done.51
  528.6 3.3 collective-permute-done.39
  535.2 3.0 collective-permute-done.46
  542.4 4.3 collective-permute-done.34
  549.4 12.4 %collective-permute-done.25 = f32[2,1024]{1,0:T(2,128)S(1)} collective-permute-done((f32[2,1024]{1,0:T(2,128)S(1)}, f32[2,1024]{1,0:T(2,128)S(1)}, u32[]{:S(2)}, u32[]{:S(2)}) %collective-permute-start.25) | collective-permute-done | bytes 8224 | tf_op jit(solution)/shard_map/ppermute | solution.py:54
  565.9 3.4 collective-permute-done.27
  (434 shorter events, 197.1 us)
Async XLA Ops:
  3.9 26.3 %collective-permute-start.2 = (bf16[512,1024]{1,0:T(8,128)(2,1)S(1)}, bf16[512,1024]{1,0:T(8,128)(2,1)}, u32[]{:S(2)}, u32[]{:S(2)}) collective-permute-start(bf16[512,1024]{1,0:T(8,128)(2,1)S(1)} %fusion.2), channel_id=1, source_target_pairs={{0,2},{1,3},{2,0},{3,1},{4,6},{5,7},{6,4},{7,5},{8,10},{9,11},{10,... | collective-permute-start | bytes 3145736 | tf_op jit(solution)/shard_map/ppermute | solution.py:54
  6.9 24.8 %collective-permute-start = (bf16[512,1024]{1,0:T(8,128)(2,1)S(1)}, bf16[512,1024]{1,0:T(8,128)(2,1)}, u32[]{:S(2)}, u32[]{:S(2)}) collective-permute-start(bf16[512,1024]{1,0:T(8,128)(2,1)S(1)} %fusion.2), channel_id=1, source_target_pairs={{0,1},{1,0},{2,3},{3,2},{4,5},{5,4},{6,7},{7,6},{8,9},{9,8},{10,11... | collective-permute-start | bytes 3145736 | tf_op jit(solution)/shard_map/ppermute | solution.py:54
  52.6 26.1 %collective-permute-start.5 = (bf16[512,1024]{1,0:T(8,128)(2,1)S(1)}, bf16[512,1024]{1,0:T(8,128)(2,1)S(1)}, u32[]{:S(2)}, u32[]{:S(2)}) collective-permute-start(bf16[512,1024]{1,0:T(8,128)(2,1)S(1)} %fusion.20), channel_id=1, source_target_pairs={{0,2},{1,3},{2,0},{3,1},{4,6},{5,7},{6,4},{7,5},{8,10},{9,11},{10,... | collective-permute-start | bytes 3145736 | tf_op jit(solution)/shard_map/ppermute | solution.py:54
  54.4 46.3 %collective-permute-start.14 = (bf16[512,1024]{1,0:T(8,128)(2,1)S(1)}, bf16[512,1024]{1,0:T(8,128)(2,1)}, u32[]{:S(2)}, u32[]{:S(2)}) collective-permute-start(bf16[512,1024]{1,0:T(8,128)(2,1)S(1)} %copy-done.12), channel_id=1, source_target_pairs={{0,2},{1,3},{2,0},{3,1},{4,6},{5,7},{6,4},{7,5},{8,10},{9,11},{10,... | collective-permute-start | bytes 3145736 | tf_op jit(solution)/shard_map/ppermute | solution.py:54
  81.9 20.5 %collective-permute-start.6 = (bf16[512,1024]{1,0:T(8,128)(2,1)}, bf16[512,1024]{1,0:T(8,128)(2,1)}, u32[]{:S(2)}, u32[]{:S(2)}) collective-permute-start(bf16[512,1024]{1,0:T(8,128)(2,1)} %multiply_convert_fusion.6), channel_id=1, source_target_pairs={{0,1},{1,0},{2,3},{3,2},{4,5},{5,4},{6,7},{7,6},{8,9},{9,8},{10,11... | collective-permute-start | bytes 3145736 | tf_op jit(solution)/shard_map/ppermute | solution.py:54
  81.9 34.1 %collective-permute-start.12 = (bf16[512,1024]{1,0:T(8,128)(2,1)S(1)}, bf16[512,1024]{1,0:T(8,128)(2,1)}, u32[]{:S(2)}, u32[]{:S(2)}) collective-permute-start(bf16[512,1024]{1,0:T(8,128)(2,1)S(1)} %copy-done.12), channel_id=1, source_target_pairs={{0,1},{1,0},{2,3},{3,2},{4,5},{5,4},{6,7},{7,6},{8,9},{9,8},{10,11... | collective-permute-start | bytes 3145736 | tf_op jit(solution)/shard_map/ppermute | solution.py:54
  100.7 71.6 %collective-permute-start.15 = (bf16[512,1024]{1,0:T(8,128)(2,1)}, bf16[512,1024]{1,0:T(8,128)(2,1)S(1)}, u32[]{:S(2)}, u32[]{:S(2)}) collective-permute-start(bf16[512,1024]{1,0:T(8,128)(2,1)} %collective-permute-done.14), channel_id=1, source_target_pairs={{0,1},{1,0},{2,3},{3,2},{4,5},{5,4},{6,7},{7,6},{8,9},{9,8},{10,11... | collective-permute-start | bytes 3145736 | tf_op jit(solution)/shard_map/ppermute | solution.py:54
  100.7 45.8 %collective-permute-start.8 = (bf16[512,1024]{1,0:T(8,128)(2,1)}, bf16[512,1024]{1,0:T(8,128)(2,1)S(1)}, u32[]{:S(2)}, u32[]{:S(2)}) collective-permute-start(bf16[512,1024]{1,0:T(8,128)(2,1)} %multiply_convert_fusion.6), channel_id=1, source_target_pairs={{0,2},{1,3},{2,0},{3,1},{4,6},{5,7},{6,4},{7,5},{8,10},{9,11},{10,... | collective-permute-start | bytes 3145736 | tf_op jit(solution)/shard_map/ppermute | solution.py:54
  132.6 285.9 %collective-permute-start.13 = (bf16[512,1024]{1,0:T(8,128)(2,1)}, bf16[512,1024]{1,0:T(8,128)(2,1)S(1)}, u32[]{:S(2)}, u32[]{:S(2)}) collective-permute-start(bf16[512,1024]{1,0:T(8,128)(2,1)} %fusion.26), channel_id=1, source_target_pairs={{0,1},{1,0},{2,3},{3,2},{4,5},{5,4},{6,7},{7,6},{8,9},{9,8},{10,11... | collective-permute-start | bytes 3145736 | tf_op jit(solution)/shard_map/ppermute | solution.py:54
  146.4 14.4 %collective-permute-start.9 = (bf16[512,1024]{1,0:T(8,128)(2,1)S(1)}, bf16[512,1024]{1,0:T(8,128)(2,1)S(1)}, u32[]{:S(2)}, u32[]{:S(2)}) collective-permute-start(bf16[512,1024]{1,0:T(8,128)(2,1)S(1)} %collective-permute-done.8), channel_id=1, source_target_pairs={{0,1},{1,0},{2,3},{3,2},{4,5},{5,4},{6,7},{7,6},{8,9},{9,8},{10,11... | collective-permute-start | bytes 3145736 | tf_op jit(solution)/shard_map/ppermute | solution.py:54
  190.0 133.2 %collective-permute-start.16 = (bf16[512,1024]{1,0:T(8,128)(2,1)}, bf16[512,1024]{1,0:T(8,128)(2,1)}, u32[]{:S(2)}, u32[]{:S(2)}) collective-permute-start(bf16[512,1024]{1,0:T(8,128)(2,1)} %fusion.27), channel_id=1, source_target_pairs={{0,1},{1,0},{2,3},{3,2},{4,5},{5,4},{6,7},{7,6},{8,9},{9,8},{10,11... | collective-permute-start | bytes 3145736 | tf_op jit(solution)/shard_map/ppermute | solution.py:54
  193.4 132.6 %collective-permute-start.10 = (bf16[512,1024]{1,0:T(8,128)(2,1)S(1)}, bf16[512,1024]{1,0:T(8,128)(2,1)S(1)}, u32[]{:S(2)}, u32[]{:S(2)}) collective-permute-start(bf16[512,1024]{1,0:T(8,128)(2,1)S(1)} %fusion.25), channel_id=1, source_target_pairs={{0,1},{1,0},{2,3},{3,2},{4,5},{5,4},{6,7},{7,6},{8,9},{9,8},{10,11... | collective-permute-start | bytes 3145736 | tf_op jit(solution)/shard_map/ppermute | solution.py:54
  199.9 16.5 %collective-permute-start.62 = (bf16[256,1152]{1,0:T(8,128)(2,1)}, bf16[256,1152]{1,0:T(8,128)(2,1)}, u32[]{:S(2)}, u32[]{:S(2)}) collective-permute-start(bf16[256,1152]{1,0:T(8,128)(2,1)} %fusion.44), channel_id=1, source_target_pairs={{0,8},{4,12},{8,0},{12,4},{16,24},{20,28},{24,16},{28,20},{1,9},{5... | collective-permute-start | bytes 1769480 | tf_op jit(solution)/shard_map/ppermute | solution.py:54
  208.7 19.6 %collective-permute-start.74 = (bf16[256,1152]{1,0:T(8,128)(2,1)}, bf16[256,1152]{1,0:T(8,128)(2,1)}, u32[]{:S(2)}, u32[]{:S(2)}) collective-permute-start(bf16[256,1152]{1,0:T(8,128)(2,1)} %fusion.46), channel_id=1, source_target_pairs={{0,8},{4,12},{8,0},{12,4},{16,24},{20,28},{24,16},{28,20},{1,9},{5... | collective-permute-start | bytes 1769480 | tf_op jit(solution)/shard_map/ppermute | solution.py:54
  216.3 15.4 %collective-permute-start.56 = (bf16[256,1152]{1,0:T(8,128)(2,1)S(1)}, bf16[256,1152]{1,0:T(8,128)(2,1)S(1)}, u32[]{:S(2)}, u32[]{:S(2)}) collective-permute-start(bf16[256,1152]{1,0:T(8,128)(2,1)S(1)} %fusion.43), channel_id=1, source_target_pairs={{0,4},{4,0},{8,12},{12,8},{16,20},{20,16},{24,28},{28,24},{1,5},{5... | collective-permute-start | bytes 1769480 | tf_op jit(solution)/shard_map/ppermute | solution.py:54
  228.3 18.3 %collective-permute-start.68 = (bf16[256,1152]{1,0:T(8,128)(2,1)S(1)}, bf16[256,1152]{1,0:T(8,128)(2,1)S(1)}, u32[]{:S(2)}, u32[]{:S(2)}) collective-permute-start(bf16[256,1152]{1,0:T(8,128)(2,1)S(1)} %fusion.45), channel_id=1, source_target_pairs={{0,4},{4,0},{8,12},{12,8},{16,20},{20,16},{24,28},{28,24},{1,5},{5... | collective-permute-start | bytes 1769480 | tf_op jit(solution)/shard_map/ppermute | solution.py:54
  246.7 21.0 %collective-permute-start.63 = (bf16[128,1152]{1,0:T(8,128)(2,1)S(1)}, bf16[128,1152]{1,0:T(8,128)(2,1)S(1)}, u32[]{:S(2)}, u32[]{:S(2)}) collective-permute-start(bf16[128,1152]{1,0:T(8,128)(2,1)S(1)} %fusion.59), channel_id=1, source_target_pairs={{0,16},{4,20},{8,24},{12,28},{16,0},{20,4},{24,8},{28,12},{1,17},{... | collective-permute-start | bytes 884744 | tf_op jit(solution)/shard_map/ppermute | solution.py:54
  265.9 14.0 %collective-permute-start.75 = (bf16[128,1152]{1,0:T(8,128)(2,1)S(1)}, bf16[128,1152]{1,0:T(8,128)(2,1)S(1)}, u32[]{:S(2)}, u32[]{:S(2)}) collective-permute-start(bf16[128,1152]{1,0:T(8,128)(2,1)S(1)} %fusion.61), channel_id=1, source_target_pairs={{0,16},{4,20},{8,24},{12,28},{16,0},{20,4},{24,8},{28,12},{1,17},{... | collective-permute-start | bytes 884744 | tf_op jit(solution)/shard_map/ppermute | solution.py:54
  280.0 15.2 %collective-permute-start.87 = (bf16[144,1024]{1,0:T(8,128)(2,1)S(1)}, bf16[144,1024]{1,0:T(8,128)(2,1)S(1)}, u32[]{:S(2)}, u32[]{:S(2)}) collective-permute-start(bf16[144,1024]{1,0:T(8,128)(2,1)S(1)} %fusion.63), channel_id=1, source_target_pairs={{0,16},{4,20},{8,24},{12,28},{16,0},{20,4},{24,8},{28,12},{1,17},{... | collective-permute-start | bytes 884744 | tf_op jit(solution)/shard_map/ppermute | solution.py:54
  280.2 18.3 %collective-permute-start.81 = (bf16[144,1024]{1,0:T(8,128)(2,1)S(1)}, bf16[144,1024]{1,0:T(8,128)(2,1)S(1)}, u32[]{:S(2)}, u32[]{:S(2)}) collective-permute-start(bf16[144,1024]{1,0:T(8,128)(2,1)S(1)} %fusion.62), channel_id=1, source_target_pairs={{0,8},{4,12},{8,0},{12,4},{16,24},{20,28},{24,16},{28,20},{1,9},{5... | collective-permute-start | bytes 884744 | tf_op jit(solution)/shard_map/ppermute | solution.py:54
  306.6 16.5 %collective-permute-start.70 = (bf16[64,1152]{1,0:T(8,128)(2,1)S(1)}, bf16[64,1152]{1,0:T(8,128)(2,1)S(1)}, u32[]{:S(2)}, u32[]{:S(2)}) collective-permute-start(bf16[64,1152]{1,0:T(8,128)(2,1)S(1)} %fusion.76), channel_id=1, source_target_pairs={{0,16},{4,20},{8,24},{12,28},{16,0},{20,4},{24,8},{28,12},{1,17},{... | collective-permute-start | bytes 442376 | tf_op jit(solution)/shard_map/ppermute | solution.py:54
  323.1 14.0 %collective-permute-start.59 = (bf16[64,1152]{1,0:T(8,128)(2,1)S(1)}, bf16[64,1152]{1,0:T(8,128)(2,1)S(1)}, u32[]{:S(2)}, u32[]{:S(2)}) collective-permute-start(bf16[64,1152]{1,0:T(8,128)(2,1)S(1)} %fusion.69), channel_id=1, source_target_pairs={{0,16},{4,20},{8,24},{12,28},{16,0},{20,4},{24,8},{28,12},{1,17},{... | collective-permute-start | bytes 442376 | tf_op jit(solution)/shard_map/ppermute | solution.py:54
  326.0 20.6 %collective-permute-start.71 = (bf16[64,1152]{1,0:T(8,128)(2,1)S(1)}, bf16[64,1152]{1,0:T(8,128)(2,1)S(1)}, u32[]{:S(2)}, u32[]{:S(2)}) collective-permute-start(bf16[64,1152]{1,0:T(8,128)(2,1)S(1)} %fusion.67), channel_id=1, source_target_pairs={{0,16},{4,20},{8,24},{12,28},{16,0},{20,4},{24,8},{28,12},{1,17},{... | collective-permute-start | bytes 442376 | tf_op jit(solution)/shard_map/ppermute | solution.py:54
  329.3 17.3 %collective-permute-start.89 = (bf16[72,1024]{1,0:T(8,128)(2,1)S(1)}, bf16[72,1024]{1,0:T(8,128)(2,1)S(1)}, u32[]{:S(2)}, u32[]{:S(2)}) collective-permute-start(bf16[72,1024]{1,0:T(8,128)(2,1)S(1)} %fusion.64), channel_id=1, source_target_pairs={{0,4},{4,0},{8,12},{12,8},{16,20},{20,16},{24,28},{28,24},{1,5},{5... | collective-permute-start | bytes 442376 | tf_op jit(solution)/shard_map/ppermute | solution.py:54
  330.4 19.4 %collective-permute-start.83 = (bf16[72,1024]{1,0:T(8,128)(2,1)S(1)}, bf16[72,1024]{1,0:T(8,128)(2,1)S(1)}, u32[]{:S(2)}, u32[]{:S(2)}) collective-permute-start(bf16[72,1024]{1,0:T(8,128)(2,1)S(1)} %fusion.65), channel_id=1, source_target_pairs={{0,16},{4,20},{8,24},{12,28},{16,0},{20,4},{24,8},{28,12},{1,17},{... | collective-permute-start | bytes 442376 | tf_op jit(solution)/shard_map/ppermute | solution.py:54
  337.1 24.5 %collective-permute-start.66 = (bf16[128,1152]{1,0:T(8,128)(2,1)S(1)}, bf16[128,1152]{1,0:T(8,128)(2,1)S(1)}, u32[]{:S(2)}, u32[]{:S(2)}) collective-permute-start(bf16[128,1152]{1,0:T(8,128)(2,1)S(1)} %maximum_select_fusion.37), channel_id=1, source_target_pairs={{0,16},{4,20},{8,24},{12,28},{16,0},{20,4},{24,8},{28,12},{1,17},{... | collective-permute-start | bytes 884744 | tf_op jit(solution)/shard_map/ppermute | solution.py:54
  346.6 28.7 %collective-permute-start.60 = (bf16[128,1152]{1,0:T(8,128)(2,1)S(1)}, bf16[128,1152]{1,0:T(8,128)(2,1)S(1)}, u32[]{:S(2)}, u32[]{:S(2)}) collective-permute-start(bf16[128,1152]{1,0:T(8,128)(2,1)S(1)} %maximum_select_fusion.36), channel_id=1, source_target_pairs={{0,8},{4,12},{8,0},{12,4},{16,24},{20,28},{24,16},{28,20},{1,9},{5... | collective-permute-start | bytes 884744 | tf_op jit(solution)/shard_map/ppermute | solution.py:54
  346.7 28.5 %collective-permute-start.78 = (bf16[128,1152]{1,0:T(8,128)(2,1)S(1)}, bf16[128,1152]{1,0:T(8,128)(2,1)S(1)}, u32[]{:S(2)}, u32[]{:S(2)}) collective-permute-start(bf16[128,1152]{1,0:T(8,128)(2,1)S(1)} %maximum_select_fusion.39), channel_id=1, source_target_pairs={{0,16},{4,20},{8,24},{12,28},{16,0},{20,4},{24,8},{28,12},{1,17},{... | collective-permute-start | bytes 884744 | tf_op jit(solution)/shard_map/ppermute | solution.py:54
  349.8 27.6 %collective-permute-start.72 = (bf16[128,1152]{1,0:T(8,128)(2,1)S(1)}, bf16[128,1152]{1,0:T(8,128)(2,1)S(1)}, u32[]{:S(2)}, u32[]{:S(2)}) collective-permute-start(bf16[128,1152]{1,0:T(8,128)(2,1)S(1)} %maximum_select_fusion.38), channel_id=1, source_target_pairs={{0,8},{4,12},{8,0},{12,4},{16,24},{20,28},{24,16},{28,20},{1,9},{5... | collective-permute-start | bytes 884744 | tf_op jit(solution)/shard_map/ppermute | solution.py:54
  361.6 19.8 %collective-permute-start.90 = (bf16[144,1024]{1,0:T(8,128)(2,1)S(1)}, bf16[144,1024]{1,0:T(8,128)(2,1)S(1)}, u32[]{:S(2)}, u32[]{:S(2)}) collective-permute-start(bf16[144,1024]{1,0:T(8,128)(2,1)S(1)} %maximum_select_fusion.41), channel_id=1, source_target_pairs={{0,16},{4,20},{8,24},{12,28},{16,0},{20,4},{24,8},{28,12},{1,17},{... | collective-permute-start | bytes 884744 | tf_op jit(solution)/shard_map/ppermute | solution.py:54
  375.3 25.0 %collective-permute-start.67 = (bf16[256,1152]{1,0:T(8,128)(2,1)S(1)}, bf16[256,1152]{1,0:T(8,128)(2,1)S(1)}, u32[]{:S(2)}, u32[]{:S(2)}) collective-permute-start(bf16[256,1152]{1,0:T(8,128)(2,1)S(1)} %maximum_select_fusion.15), channel_id=1, source_target_pairs={{0,8},{4,12},{8,0},{12,4},{16,24},{20,28},{24,16},{28,20},{1,9},{5... | collective-permute-start | bytes 1769480 | tf_op jit(solution)/shard_map/ppermute | solution.py:54
  377.5 24.8 %collective-permute-start.61 = (bf16[256,1152]{1,0:T(8,128)(2,1)S(1)}, bf16[256,1152]{1,0:T(8,128)(2,1)S(1)}, u32[]{:S(2)}, u32[]{:S(2)}) collective-permute-start(bf16[256,1152]{1,0:T(8,128)(2,1)S(1)} %maximum_select_fusion.14), channel_id=1, source_target_pairs={{0,4},{4,0},{8,12},{12,8},{16,20},{20,16},{24,28},{28,24},{1,5},{5... | collective-permute-start | bytes 1769480 | tf_op jit(solution)/shard_map/ppermute | solution.py:54
  381.3 37.2 %collective-permute-start.17 = (bf16[512,1024]{1,0:T(8,128)(2,1)S(1)}, bf16[512,1024]{1,0:T(8,128)(2,1)S(1)}, u32[]{:S(2)}, u32[]{:S(2)}) collective-permute-start(bf16[512,1024]{1,0:T(8,128)(2,1)S(1)} %fusion.14), channel_id=1, source_target_pairs={{0,2},{1,3},{2,0},{3,1},{4,6},{5,7},{6,4},{7,5},{8,10},{9,11},{10,... | collective-permute-start | bytes 3145736 | tf_op jit(solution)/shard_map/ppermute | solution.py:54
  387.7 25.3 %collective-permute-start.79 = (bf16[256,1152]{1,0:T(8,128)(2,1)S(1)}, bf16[256,1152]{1,0:T(8,128)(2,1)S(1)}, u32[]{:S(2)}, u32[]{:S(2)}) collective-permute-start(bf16[256,1152]{1,0:T(8,128)(2,1)S(1)} %maximum_select_fusion.17), channel_id=1, source_target_pairs={{0,8},{4,12},{8,0},{12,4},{16,24},{20,28},{24,16},{28,20},{1,9},{5... | collective-permute-start | bytes 1769480 | tf_op jit(solution)/shard_map/ppermute | solution.py:54
  400.3 15.2 %collective-permute-start.73 = (bf16[256,1152]{1,0:T(8,128)(2,1)S(1)}, bf16[256,1152]{1,0:T(8,128)(2,1)S(1)}, u32[]{:S(2)}, u32[]{:S(2)}) collective-permute-start(bf16[256,1152]{1,0:T(8,128)(2,1)S(1)} %maximum_select_fusion.16), channel_id=1, source_target_pairs={{0,4},{4,0},{8,12},{12,8},{16,20},{20,16},{24,28},{28,24},{1,5},{5... | collective-permute-start | bytes 1769480 | tf_op jit(solution)/shard_map/ppermute | solution.py:54
  402.3 23.2 %collective-permute-start.91 = (bf16[288,1024]{1,0:T(8,128)(2,1)S(1)}, bf16[288,1024]{1,0:T(8,128)(2,1)S(1)}, u32[]{:S(2)}, u32[]{:S(2)}) collective-permute-start(bf16[288,1024]{1,0:T(8,128)(2,1)S(1)} %maximum_select_fusion.19), channel_id=1, source_target_pairs={{0,8},{4,12},{8,0},{12,4},{16,24},{20,28},{24,16},{28,20},{1,9},{5... | collective-permute-start | bytes 1769480 | tf_op jit(solution)/shard_map/ppermute | solution.py:54
  412.9 15.2 %collective-permute-start.85 = (bf16[288,1024]{1,0:T(8,128)(2,1)S(1)}, bf16[288,1024]{1,0:T(8,128)(2,1)S(1)}, u32[]{:S(2)}, u32[]{:S(2)}) collective-permute-start(bf16[288,1024]{1,0:T(8,128)(2,1)S(1)} %maximum_select_fusion.18), channel_id=1, source_target_pairs={{0,4},{4,0},{8,12},{12,8},{16,20},{20,16},{24,28},{28,24},{1,5},{5... | collective-permute-start | bytes 1769480 | tf_op jit(solution)/shard_map/ppermute | solution.py:54
  420.1 25.7 %collective-permute-start.18 = (bf16[512,1024]{1,0:T(8,128)(2,1)S(1)}, bf16[512,1024]{1,0:T(8,128)(2,1)S(1)}, u32[]{:S(2)}, u32[]{:S(2)}) collective-permute-start(bf16[512,1024]{1,0:T(8,128)(2,1)S(1)} %fusion.109), channel_id=1, source_target_pairs={{0,1},{1,0},{2,3},{3,2},{4,5},{5,4},{6,7},{7,6},{8,9},{9,8},{10,11... | collective-permute-start | bytes 3145736 | tf_op jit(solution)/shard_map/ppermute | solution.py:54
  420.2 25.6 %collective-permute-start.20 = (bf16[512,1024]{1,0:T(8,128)(2,1)S(1)}, bf16[512,1024]{1,0:T(8,128)(2,1)S(1)}, u32[]{:S(2)}, u32[]{:S(2)}) collective-permute-start(bf16[512,1024]{1,0:T(8,128)(2,1)S(1)} %fusion.109), channel_id=1, source_target_pairs={{0,2},{1,3},{2,0},{3,1},{4,6},{5,7},{6,4},{7,5},{8,10},{9,11},{10,... | collective-permute-start | bytes 3145736 | tf_op jit(solution)/shard_map/ppermute | solution.py:54
  456.0 63.3 %collective-permute-start.22 = (bf16[512,1024]{1,0:T(8,128)(2,1)S(1)}, bf16[512,1024]{1,0:T(8,128)(2,1)S(1)}, u32[]{:S(2)}, u32[]{:S(2)}) collective-permute-start(bf16[512,1024]{1,0:T(8,128)(2,1)S(1)} %fusion.29), channel_id=1, source_target_pairs={{0,1},{1,0},{2,3},{3,2},{4,5},{5,4},{6,7},{7,6},{8,9},{9,8},{10,11... | collective-permute-start | bytes 3145736 | tf_op jit(solution)/shard_map/ppermute | solution.py:54
  458.6 82.6 %collective-permute-start.19 = (bf16[512,1024]{1,0:T(8,128)(2,1)S(1)}, bf16[512,1024]{1,0:T(8,128)(2,1)S(1)}, u32[]{:S(2)}, u32[]{:S(2)}) collective-permute-start(bf16[512,1024]{1,0:T(8,128)(2,1)S(1)} %fusion.28), channel_id=1, source_target_pairs={{0,1},{1,0},{2,3},{3,2},{4,5},{5,4},{6,7},{7,6},{8,9},{9,8},{10,11... | collective-permute-start | bytes 3145736 | tf_op jit(solution)/shard_map/ppermute | solution.py:54
  467.5 19.3 %collective-permute-start.41 = (bf16[512,256]{1,0:T(8,128)(2,1)S(1)}, bf16[512,256]{1,0:T(8,128)(2,1)S(1)}, u32[]{:S(2)}, u32[]{:S(2)}) collective-permute-start(bf16[512,256]{1,0:T(8,128)(2,1)S(1)} %fusion.72), channel_id=1, source_target_pairs={{0,4},{4,0},{8,12},{12,8},{16,20},{20,16},{24,28},{28,24},{1,5},{5... | collective-permute-start | bytes 786440 | tf_op jit(solution)/shard_map/ppermute | solution.py:54
  469.1 17.7 %collective-permute-start.35 = (bf16[512,256]{1,0:T(8,128)(2,1)S(1)}, bf16[512,256]{1,0:T(8,128)(2,1)S(1)}, u32[]{:S(2)}, u32[]{:S(2)}) collective-permute-start(bf16[512,256]{1,0:T(8,128)(2,1)S(1)} %fusion.71), channel_id=1, source_target_pairs={{0,8},{4,12},{8,0},{12,4},{16,24},{20,28},{24,16},{28,20},{1,9},{5... | collective-permute-start | bytes 786440 | tf_op jit(solution)/shard_map/ppermute | solution.py:54
  522.1 19.2 %collective-permute-start.23 = (bf16[512,1024]{1,0:T(8,128)(2,1)S(1)}, bf16[512,1024]{1,0:T(8,128)(2,1)S(1)}, u32[]{:S(2)}, u32[]{:S(2)}) collective-permute-start(bf16[512,1024]{1,0:T(8,128)(2,1)S(1)} %fusion.12), channel_id=1, source_target_pairs={{0,2},{1,3},{2,0},{3,1},{4,6},{5,7},{6,4},{7,5},{8,10},{9,11},{10,... | collective-permute-start | bytes 3145736 | tf_op jit(solution)/shard_map/ppermute | solution.py:54
  535.2 35.0 %collective-permute-start.7 = (bf16[512,1024]{1,0:T(8,128)(2,1)S(1)}, bf16[512,1024]{1,0:T(8,128)(2,1)S(1)}, u32[]{:S(2)}, u32[]{:S(2)}) collective-permute-start(bf16[512,1024]{1,0:T(8,128)(2,1)S(1)} %copy-done.27), channel_id=1, source_target_pairs={{0,1},{1,0},{2,3},{3,2},{4,5},{5,4},{6,7},{7,6},{8,9},{9,8},{10,11... | collective-permute-start | bytes 3145736 | tf_op jit(solution)/shard_map/ppermute | solution.py:54
  538.3 31.9 %collective-permute-start.11 = (bf16[512,1024]{1,0:T(8,128)(2,1)S(1)}, bf16[512,1024]{1,0:T(8,128)(2,1)S(1)}, u32[]{:S(2)}, u32[]{:S(2)}) collective-permute-start(bf16[512,1024]{1,0:T(8,128)(2,1)S(1)} %fusion.16), channel_id=1, source_target_pairs={{0,2},{1,3},{2,0},{3,1},{4,6},{5,7},{6,4},{7,5},{8,10},{9,11},{10,... | collective-permute-start | bytes 3145736 | tf_op jit(solution)/shard_map/ppermute | solution.py:54
  541.2 21.1 %collective-permute-start.55 = (bf16[128,1024]{1,0:T(8,128)(2,1)S(1)}, bf16[128,1024]{1,0:T(8,128)(2,1)S(1)}, u32[]{:S(2)}, u32[]{:S(2)}) collective-permute-start(bf16[128,1024]{1,0:T(8,128)(2,1)S(1)} %maximum_select_fusion.45), channel_id=1, source_target_pairs={{0,8},{4,12},{8,0},{12,4},{16,24},{20,28},{24,16},{28,20},{1,9},{5... | collective-permute-start | bytes 786440 | tf_op jit(solution)/shard_map/ppermute | solution.py:54
  546.9 14.9 %collective-permute-start.25 = (f32[2,1024]{1,0:T(2,128)S(1)}, f32[2,1024]{1,0:T(2,128)S(1)}, u32[]{:S(2)}, u32[]{:S(2)}) collective-permute-start(f32[2,1024]{1,0:T(2,128)S(1)} %fusion.106), channel_id=1, source_target_pairs={{0,2},{1,3},{2,0},{3,1},{4,6},{5,7},{6,4},{7,5},{8,10},{9,11},{10,... | collective-permute-start | bytes 24584 | tf_op jit(solution)/shard_map/ppermute | solution.py:54
  (107 other events, 955.5 us)

commit v2 on v1

--- a/solution.py
+++ b/solution.py
@@ -3,9 +3,12 @@
 import jax
 import jax.numpy as jnp
 from jax import lax
+from jax.experimental import pallas as pl
+from jax.experimental.pallas import tpu as pltpu
 from jax.sharding import PartitionSpec as P
 
 LEN = 1024
+ROWS = 512
 F32 = jnp.float32
 BF16 = jnp.bfloat16
 
@@ -30,6 +33,88 @@
 
 def dot_cols(a, b):
     return lax.dot_general(a, b, (((1,), (1,)), ((), ())), preferred_element_type=F32)
+
+
+def after(value, *others):
+    return lax.optimization_barrier((value, *others))[0]
+
+
+def mlp_kernel(
+    second_ref,
+    cot_ref,
+    gate_ref,
+    up_ref,
+    down_ref,
+    out_ref,
+    back_ref,
+    gate_grad_ref,
+    up_grad_ref,
+    down_grad_ref,
+    gate_sum,
+    up_sum,
+    down_sum,
+):
+    step = pl.program_id(0)
+    second, cot = second_ref[...], cot_ref[...]
+    gate = dot(second, gate_ref[...])
+    upper = dot(second, up_ref[...])
+    sigma = jax.nn.sigmoid(gate)
+    active = gate * sigma
+    hidden = (active * upper).astype(BF16)
+    out_ref[...] = dot(hidden, down_ref[...]).astype(BF16)
+    hidden_grad = dot_cols(cot, down_ref[...])
+    gate_grad = (hidden_grad * upper * sigma * (1.0 + gate * (1.0 - sigma))).astype(BF16)
+    up_grad = (hidden_grad * active).astype(BF16)
+    back_ref[...] = (dot_cols(gate_grad, gate_ref[...]) + dot_cols(up_grad, up_ref[...])).astype(BF16)
+    parts = (
+        (gate_sum, dot_rows(second, gate_grad)),
+        (up_sum, dot_rows(second, up_grad)),
+        (down_sum, dot_rows(hidden, cot)),
+    )
+
+    @pl.when(step == 0)
+    def _():
+        for total, part in parts:
+            total[...] = part
+
+    @pl.when(step > 0)
+    def _():
+        for total, part in parts:
+            total[...] += part
+
+    @pl.when(step == pl.num_programs(0) - 1)
+    def _():
+        gate_grad_ref[...] = gate_sum[...].astype(BF16)
+        up_grad_ref[...] = up_sum[...].astype(BF16)
+        down_grad_ref[...] = down_sum[...].astype(BF16)
+
+
+def mlp(second, cot, gate_weight, up_weight, down_weight):
+    rows, width = second.shape
+    units = gate_weight.shape[1]
+    tile = min(ROWS, rows)
+    by_rows = pl.BlockSpec((tile, width), lambda i: (i, 0))
+
+    def whole(shape):
+        return pl.BlockSpec(shape, lambda i: (0, 0), pipeline_mode=pl.Buffered(1))
+
+    wide, tall = (width, units), (units, width)
+    return pl.pallas_call(
+        mlp_kernel,
+        grid=(rows // tile,),
+        in_specs=[by_rows, by_rows, whole(wide), whole(wide), whole(tall)],
+        out_specs=[by_rows, by_rows, whole(wide), whole(wide), whole(tall)],
+        out_shape=[jax.ShapeDtypeStruct((rows, width), BF16)] * 2
+        + [jax.ShapeDtypeStruct(wide, BF16)] * 2
+        + [jax.ShapeDtypeStruct(tall, BF16)],
+        scratch_shapes=[pltpu.VMEM(wide, F32), pltpu.VMEM(wide, F32), pltpu.VMEM(tall, F32)],
+        compiler_params=pltpu.CompilerParams(vmem_limit_bytes=56 << 20),
+        cost_estimate=pl.CostEstimate(
+            flops=18 * rows * width * units,
+            bytes_accessed=12 * width * units + 8 * rows * width,
+            transcendentals=rows * units,
+        ),
+    )(second, cot, gate_weight, up_weight, down_weight)
 
 
 def body(
@@ -70,27 +155,32 @@
 
     def scatter(mine, other):
         keep, give = parted(core, other)
-        total = keep + swap(give.astype(BF16), "tensor", 1).astype(F32)
-        got_far = swap(total.astype(BF16), "tensor", 2)
+        total = keep.astype(F32) + swap(give.astype(BF16), "tensor", 1).astype(F32)
+        total = total.astype(BF16)
+        got_far = swap(total, "tensor", 2)
         keep, give = parted(core, mine)
-        return keep + swap(give.astype(BF16), "tensor", 1).astype(F32) + got_far.astype(F32)
+        near = keep.astype(F32) + swap(give.astype(BF16), "tensor", 1).astype(F32)
+        return near + got_far.astype(F32), total
 
     dp_bits = [1 << k for k in range(n_dp.bit_length() - 1)]
 
-    def sum_dp(value, turn):
-        bits = dp_bits[turn:] + dp_bits[:turn]
+    def order_of(turn):
+        return dp_bits[turn:] + dp_bits[:turn]
+
+    def reduce_dp(value, turn=0):
         current = value
-        for bit in bits:
+        for bit in order_of(turn):
             keep, give = parted((dp_at // bit) % 2, current)
             current = keep + swap(give.astype(BF16), "dp", bit).astype(F32)
-        current = current.astype(BF16)
-        for bit in reversed(bits):
+        return current.astype(BF16)
+
+    def spread_dp(current, turn=0):
+        for bit in reversed(order_of(turn)):
             current = ordered((dp_at // bit) % 2, current, swap(current, "dp", bit))
         return current.astype(F32)
 
-    def sum_dp_split(value):
-        half = value.shape[0] // 2
-        return jnp.concatenate([sum_dp(value[:half], 0), sum_dp(value[half:], 1)])
+    def sum_dp(value, turn=0):
+        return spread_dp(reduce_dp(value, turn), turn)
 
     def sum_small(value, axis):
         bit = 1
@@ -133,42 +223,37 @@
         ).astype(BF16)
         return stream_grad, conv_grad, dot_cols(stream_grad, in_flat)
 
-    def mlp_forward(second):
-        gate = dot(second, gate_weight)
-        upper = dot(second, up_weight)
-        hidden = (gate * jax.nn.sigmoid(gate) * upper).astype(BF16)
-        return gate, upper, hidden
-
-    def mlp_backward(gate, upper, cotangent):
-        hidden_grad = dot_cols(cotangent, down_weight)
-        sigma = jax.nn.sigmoid(gate)
-        gate_grad = (hidden_grad * upper * sigma * (1.0 + gate * (1.0 - sigma))).astype(BF16)
-        up_grad = (hidden_grad * gate * sigma).astype(BF16)
-        return gate_grad, up_grad, dot_cols(gate_grad, gate_weight) + dot_cols(up_grad, up_weight)
-
     inputs = tokens.astype(F32)
     scale_one = rms_scale(inputs)
     first_m, first_o = gather((inputs * scale_one * mixer_gain).astype(BF16))
+    cot_m, cot_o = gather(after(out_grad, first_o))
     kept_o, part_o = conv_forward(first_o)
     kept_m, part_m = conv_forward(first_m)
-    middle = inputs + scatter(part_m, part_o)
+    middle = inputs + scatter(part_m, part_o)[0]
     scale_two = rms_scale(middle)
     second_m, second_o = gather((middle * scale_two * mlp_gain).astype(BF16))
-    cot_m, cot_o = gather(out_grad)
-    gate_m, upper_m, hidden_m = mlp_forward(second_m)
-    gate_o, upper_o, hidden_o = mlp_forward(second_o)
-    down_grad = sum_dp_split(dot_rows(hidden_m, cot_m) + dot_rows(hidden_o, cot_o))
-    output = (middle + scatter(dot(hidden_m, down_weight), dot(hidden_o, down_weight))).astype(BF16)
-
-    gate_grad_o, up_grad_o, back_o = mlp_backward(gate_o, upper_o, cot_o)
-    gate_grad_m, up_grad_m, back_m = mlp_backward(gate_m, upper_m, cot_m)
-    second_grad = scatter(back_m, back_o)
-    gate_w_grad = sum_dp_split(dot_rows(second_m, gate_grad_m) + dot_rows(second_o, gate_grad_o))
-    up_w_grad = sum_dp_split(dot_rows(second_m, up_grad_m) + dot_rows(second_o, up_grad_o))
+    out_m, back_m, *w_grads_m = mlp(second_m, cot_m, gate_weight, up_weight, down_weight)
+    out_o, back_o, *w_grads_o = mlp(second_o, cot_o, gate_weight, up_weight, down_weight)
+    second_grad, sent = scatter(back_m, back_o)
+
+    halves = []
+    for grad_m, grad_o in zip(w_grads_m, w_grads_o):
+        half = grad_m.shape[0] // 2
+        for rows in (slice(0, half), slice(half, None)):
+            halves.append(grad_m[rows].astype(F32) + grad_o[rows].astype(F32))
+    pieces = [reduce_dp(half) for half in halves[:2]]
+    pieces += [reduce_dp(after(half, sent)) for half in halves[2:4]]
 
     mlp_gain_part = jnp.sum(second_grad * middle * scale_two, axis=0)
     middle_grad = out_grad.astype(F32) + norm_back(second_grad, middle, scale_two, mlp_gain)
     branch_m, branch_o = gather(middle_grad.astype(BF16))
+    pieces += [reduce_dp(after(half, branch_o)) for half in halves[4:]]
+    sums = [spread_dp(after(piece, branch_o)) for piece in pieces]
+    gate_w_grad, up_w_grad, down_grad = (
+        jnp.concatenate(sums[k : k + 2]) for k in range(0, 6, 2)
+    )
+    output = (middle + scatter(after(out_m, branch_o), after(out_o, branch_o))[0]).astype(BF16)
+
     out_w_grad = sum_dp(dot_rows(kept_m[5], branch_m) + dot_rows(kept_o[5], branch_o), 1)
     stream_grad_o, conv_grad_o, back_o = conv_backward(kept_o, branch_o)
     stream_grad_m, conv_grad_m, back_m = conv_backward(kept_m, branch_m)
@@ -176,7 +261,7 @@
     in_w_grad = jnp.stack(
         [sum_dp(in_flat_grad[:, k * chans : (k + 1) * chans], k % 2) for k in range(3)]
     )
-    first_grad = scatter(back_m, back_o)
+    first_grad = scatter(back_m, back_o)[0]
     mixer_gain_part = jnp.sum(first_grad * inputs * scale_one, axis=0)
     input_grad = (middle_grad + norm_back(first_grad, inputs, scale_one, mixer_gain)).astype(BF16)
 

time: 584 us -> 613 us (1.050)
  matrix products: 128 us -> 22.4 us
  Pallas kernels: 0 us -> 72.5 us
  starting transfers between devices: 89.8 us -> 121 us
  other arithmetic: 39.9 us -> 66.8 us
  waiting for transfers between devices: 294 us -> 301 us
    pallas_call x0 -> x2, Pallas kernels: none -> 72.5 us  [mlp(): pl.pallas_call(mlp_kernel, grid=(rows // tile,), in_specs=[by_rows, by_ro...]
    dot_general x10 -> x4, matrix products: 48.6 us -> 8.94 us  [dot_rows(): lax.dot_general(a, b, (((0,), (0,)), ((), ())), preferred_element_type=F32)]
    dot_general x10 -> x4, matrix products: 41.4 us -> 7.74 us  [dot(): return jnp.dot(a, b, preferred_element_type=F32)]
    dot_general x10 -> x4, matrix products: 37.6 us -> 5.75 us  [dot_cols(): lax.dot_general(a, b, (((1,), (1,)), ((), ())), preferred_element_type=F32)]
    ppermute x92, starting transfers between devices: 89.8 us -> 121 us  [swap(): return lax.ppermute(value, axis, [(i, i ^ bit) for i in range(size[axis])])]
    select_n x29 -> x35, other arithmetic: 5.25 us -> 28.1 us  [ordered(): jnp.where(side == 0, jnp.concatenate([own, other]), jnp.concatenate([othe...]
    ppermute x92, waiting for transfers between devices: 294 us -> 301 us  [swap(): return lax.ppermute(value, axis, [(i, i ^ bit) for i in range(size[axis])])]
  transfers between devices with their start and end apart: 92 -> 92, of which waited for: 51 -> 55; matrix products, arithmetic and copies ran while one was open for 28% -> 13% of each run, Pallas kernels for 0% -> 12%
where the time goes in v2:
time: 613 us; the launch traced here: 603 us
  waiting for transfers between devices  301 us (49%)
  starting transfers between devices  121 us (20%)
  Pallas kernels  72.5 us (12%)
  other arithmetic  66.8 us (11%)
  matrix products  22.4 us (4%)
  local copies, waits for them, and re-layouts  17.7 us (3%)
    ppermute x92, waiting for transfers between devices, swap(): return lax.ppermute(value, axis, [(i, i ^ bit) for i in range(size[axis])])  301 us
    ppermute x92, starting transfers between devices, swap(): return lax.ppermute(value, axis, [(i, i ^ bit) for i in range(size[axis])])  121 us
    pallas_call x2, Pallas kernels, mlp(): pl.pallas_call(mlp_kernel, grid=(rows // tile,), in_specs=[by_rows, by_ro...  72.5 us
    select_n x35, other arithmetic, ordered(): jnp.where(side == 0, jnp.concatenate([own, other]), jnp.concatenate([othe...  28.1 us
  transfers between devices with their start and end apart: 92, of which 55 were waited for; matrix products, arithmetic and copies ran while one was open for 13% of the time, Pallas kernels for 12%

profile of v2, /device:TPU:0, one launch (start us, length us, event | category | flops | bytes accessed | tf_op | source)
XLA Modules:
  0.0 603.4 jit_solution(4720741433259074480)
XLA Ops:
  7.8 23.4 %collective-permute-done.2 = bf16[512,1024]{1,0:T(8,128)(2,1)S(1)} collective-permute-done((bf16[512,1024]{1,0:T(8,128)(2,1)}, bf16[512,1024]{1,0:T(8,128)(2,1)S(1)}, u32[]{:S(2)}, u32[]{:S(2)}) %collective-permute-start.2) | collective-permute-done | bytes 1048608 | tf_op jit(solution)/shard_map/ppermute | solution.py:139
  31.4 4.5 fusion.46
  36.1 3.9 maximum_select_fusion.1
  53.7 22.5 %collective-permute-done.11 = bf16[512,1024]{1,0:T(8,128)(2,1)} collective-permute-done((bf16[512,1024]{1,0:T(8,128)(2,1)}, bf16[512,1024]{1,0:T(8,128)(2,1)}, u32[]{:S(2)}, u32[]{:S(2)}) %collective-permute-start.11) | collective-permute-done | bytes 1048608 | tf_op jit(solution)/shard_map/ppermute | solution.py:139
  76.2 21.9 %collective-permute-done.5 = bf16[512,1024]{1,0:T(8,128)(2,1)S(1)} collective-permute-done((bf16[512,1024]{1,0:T(8,128)(2,1)S(1)}, bf16[512,1024]{1,0:T(8,128)(2,1)S(1)}, u32[]{:S(2)}, u32[]{:S(2)}) %collective-permute-start.5) | collective-permute-done | bytes 1048608 | tf_op jit(solution)/shard_map/ppermute | solution.py:139
  101.7 4.6 maximum_select_fusion.3.cot_ref
  106.3 4.7 maximum_select_fusion.5.cot_ref
  111.0 14.0 %collective-permute-done.9 = bf16[512,1024]{1,0:T(8,128)(2,1)} collective-permute-done((bf16[512,1024]{1,0:T(8,128)(2,1)}, bf16[512,1024]{1,0:T(8,128)(2,1)}, u32[]{:S(2)}, u32[]{:S(2)}) %collective-permute-start.9) | collective-permute-done | bytes 1048608 | tf_op jit(solution)/shard_map/ppermute | solution.py:139
  125.0 4.7 maximum_select_fusion.2.second_ref
  129.7 36.0 %shard_map.177 = (bf16[1024,1024]{1,0:T(8,128)(2,1)}, bf16[1024,1024]{1,0:T(8,128)(2,1)}, bf16[1024,1152]{1,0:T(8,128)(2,1)}, bf16[1024,1152]{1,0:T(8,128)(2,1)}, bf16[1152,1024]{1,0:T(8,128)(2,1)}) custom-call(bf16[1024,1024]{1,0:T(8,128)(2,1)} %maximum_select_fusion.2.second_ref, bf16[1024,1024]{1,0:T(8,128)(2,1)} %maximum_select_fusion.3.cot_ref, ...), custom_call_target="tpu_custom_call" | custom-call | flops 21743271936 | bytes 22544384 | tf_op jit(solution)/shard_map/pallas_call | solution.py:102
  168.6 3.9 maximum_select_fusion.4.second_ref
  172.5 36.4 %shard_map.178 = (bf16[1024,1024]{1,0:T(8,128)(2,1)}, bf16[1024,1024]{1,0:T(8,128)(2,1)}, bf16[1024,1152]{1,0:T(8,128)(2,1)}, bf16[1024,1152]{1,0:T(8,128)(2,1)}, bf16[1152,1024]{1,0:T(8,128)(2,1)}) custom-call(bf16[1024,1024]{1,0:T(8,128)(2,1)} %maximum_select_fusion.4.second_ref, bf16[1024,1024]{1,0:T(8,128)(2,1)} %maximum_select_fusion.5.cot_ref, ...), custom_call_target="tpu_custom_call" | custom-call | flops 21743271936 | bytes 22544384 | tf_op jit(solution)/shard_map/pallas_call | solution.py:102
  210.3 3.6 convert_add_fusion.4
  217.3 12.9 %collective-permute-done.62 = bf16[256,1152]{1,0:T(8,128)(2,1)S(1)} collective-permute-done((bf16[256,1152]{1,0:T(8,128)(2,1)S(1)}, bf16[256,1152]{1,0:T(8,128)(2,1)S(1)}, u32[]{:S(2)}, u32[]{:S(2)}) %collective-permute-start.62) | collective-permute-done | bytes 589856 | tf_op jit(solution)/shard_map/ppermute | solution.py:139
  232.3 10.2 %collective-permute-done.56 = bf16[256,1152]{1,0:T(8,128)(2,1)S(1)} collective-permute-done((bf16[256,1152]{1,0:T(8,128)(2,1)S(1)}, bf16[256,1152]{1,0:T(8,128)(2,1)S(1)}, u32[]{:S(2)}, u32[]{:S(2)}) %collective-permute-start.56) | collective-permute-done | bytes 589856 | tf_op jit(solution)/shard_map/ppermute | solution.py:139
  247.3 7.3 %collective-permute-done.57 = bf16[128,1152]{1,0:T(8,128)(2,1)S(1)} collective-permute-done((bf16[128,1152]{1,0:T(8,128)(2,1)S(1)}, bf16[128,1152]{1,0:T(8,128)(2,1)S(1)}, u32[]{:S(2)}, u32[]{:S(2)}) %collective-permute-start.57) | collective-permute-done | bytes 294944 | tf_op jit(solution)/shard_map/ppermute | solution.py:139
  258.7 4.7 collective-permute-done.58
  266.7 6.7 %collective-permute-done.74 = bf16[256,1152]{1,0:T(8,128)(2,1)S(1)} collective-permute-done((bf16[256,1152]{1,0:T(8,128)(2,1)S(1)}, bf16[256,1152]{1,0:T(8,128)(2,1)S(1)}, u32[]{:S(2)}, u32[]{:S(2)}) %collective-permute-start.74) | collective-permute-done | bytes 589856 | tf_op jit(solution)/shard_map/ppermute | solution.py:139
  276.2 7.4 %collective-permute-done.68 = bf16[256,1152]{1,0:T(8,128)(2,1)S(1)} collective-permute-done((bf16[256,1152]{1,0:T(8,128)(2,1)S(1)}, bf16[256,1152]{1,0:T(8,128)(2,1)S(1)}, u32[]{:S(2)}, u32[]{:S(2)}) %collective-permute-start.68) | collective-permute-done | bytes 589856 | tf_op jit(solution)/shard_map/ppermute | solution.py:139
  294.5 19.2 %collective-permute-done.15 = bf16[512,1024]{1,0:T(8,128)(2,1)S(1)} collective-permute-done((bf16[512,1024]{1,0:T(8,128)(2,1)S(1)}, bf16[512,1024]{1,0:T(8,128)(2,1)S(1)}, u32[]{:S(2)}, u32[]{:S(2)}) %collective-permute-start.15) | collective-permute-done | bytes 1048608 | tf_op jit(solution)/shard_map/ppermute | solution.py:139
  333.4 4.4 fusion.37
  344.4 4.6 collective-permute-done.47
  350.0 3.0 collective-permute-done.48
  362.2 3.7 collective-permute-done.59
  368.9 3.7 collective-permute-done.77
  375.0 3.9 collective-permute-done.71
  383.4 4.7 collective-permute-done.29
  391.6 6.1 %collective-permute-done.42 = bf16[256,256]{1,0:T(8,128)(2,1)S(1)} collective-permute-done((bf16[256,256]{1,0:T(8,128)(2,1)S(1)}, bf16[256,256]{1,0:T(8,128)(2,1)S(1)}, u32[]{:S(2)}, u32[]{:S(2)}) %collective-permute-start.42) | collective-permute-done | bytes 131104 | tf_op jit(solution)/shard_map/ppermute | solution.py:139
  397.7 3.1 collective-permute-start.36
  403.7 5.0 collective-permute-start.30
  408.8 3.9 collective-permute-done.30
  412.7 3.7 collective-permute-start.51
  416.4 3.9 collective-permute-done.51
  423.1 5.1 collective-permute-done.60
  463.0 4.2 collective-permute-done.32
  468.9 3.3 collective-permute-done.38
  473.9 3.2 collective-permute-done.53
  493.5 3.2 collective-permute-done.87
  496.8 3.1 collective-permute-done.81
  515.1 5.8 collective-permute-done.82
  520.9 3.2 collective-permute-start.79
  525.3 12.2 %collective-permute-done.79 = bf16[256,1152]{1,0:T(8,128)(2,1)S(1)} collective-permute-done((bf16[256,1152]{1,0:T(8,128)(2,1)S(1)}, bf16[256,1152]{1,0:T(8,128)(2,1)S(1)}, u32[]{:S(2)}, u32[]{:S(2)}) %collective-permute-start.79) | collective-permute-done | bytes 589856 | tf_op jit(solution)/shard_map/ppermute | solution.py:139
  540.4 4.2 collective-permute-done.73
  549.4 3.0 collective-permute-done.83
  552.7 5.3 collective-permute-done.90
  571.2 9.8 %collective-permute-done.85 = bf16[288,1024]{1,0:T(8,128)(2,1)S(1)} collective-permute-done((bf16[288,1024]{1,0:T(8,128)(2,1)S(1)}, bf16[288,1024]{1,0:T(8,128)(2,1)S(1)}, u32[]{:S(2)}, u32[]{:S(2)}) %collective-permute-start.85) | collective-permute-done | bytes 589856 | tf_op jit(solution)/shard_map/ppermute | solution.py:139
  586.0 4.5 collective-permute-done.25
  590.9 3.3 collective-permute-done.26
  (391 shorter events, 221.0 us)
Async XLA Ops:
  4.9 26.3 %collective-permute-start.2 = (bf16[512,1024]{1,0:T(8,128)(2,1)}, bf16[512,1024]{1,0:T(8,128)(2,1)S(1)}, u32[]{:S(2)}, u32[]{:S(2)}) collective-permute-start(bf16[512,1024]{1,0:T(8,128)(2,1)} %fusion.2), channel_id=1, source_target_pairs={{0,2},{1,3},{2,0},{3,1},{4,6},{5,7},{6,4},{7,5},{8,10},{9,11},{10,... | collective-permute-start | bytes 3145736 | tf_op jit(solution)/shard_map/ppermute | solution.py:139
  7.8 23.6 %collective-permute-start = (bf16[512,1024]{1,0:T(8,128)(2,1)}, bf16[512,1024]{1,0:T(8,128)(2,1)}, u32[]{:S(2)}, u32[]{:S(2)}) collective-permute-start(bf16[512,1024]{1,0:T(8,128)(2,1)} %fusion.2), channel_id=1, source_target_pairs={{0,1},{1,0},{2,3},{3,2},{4,5},{5,4},{6,7},{7,6},{8,9},{9,8},{10,11... | collective-permute-start | bytes 3145736 | tf_op jit(solution)/shard_map/ppermute | solution.py:139
  49.7 26.4 %collective-permute-start.1 = (bf16[512,1024]{1,0:T(8,128)(2,1)S(1)}, bf16[512,1024]{1,0:T(8,128)(2,1)S(1)}, u32[]{:S(2)}, u32[]{:S(2)}) collective-permute-start(bf16[512,1024]{1,0:T(8,128)(2,1)S(1)} %fusion.22), channel_id=1, source_target_pairs={{0,1},{1,0},{2,3},{3,2},{4,5},{5,4},{6,7},{7,6},{8,9},{9,8},{10,11... | collective-permute-start | bytes 3145736 | tf_op jit(solution)/shard_map/ppermute | solution.py:139
  49.8 26.3 %collective-permute-start.11 = (bf16[512,1024]{1,0:T(8,128)(2,1)}, bf16[512,1024]{1,0:T(8,128)(2,1)}, u32[]{:S(2)}, u32[]{:S(2)}) collective-permute-start(bf16[512,1024]{1,0:T(8,128)(2,1)} %param.19), channel_id=1, source_target_pairs={{0,2},{1,3},{2,0},{3,1},{4,6},{5,7},{6,4},{7,5},{8,10},{9,11},{10,... | collective-permute-start | bytes 3145736 | tf_op jit(solution)/shard_map/ppermute | solution.py:139
  52.1 46.0 %collective-permute-start.5 = (bf16[512,1024]{1,0:T(8,128)(2,1)S(1)}, bf16[512,1024]{1,0:T(8,128)(2,1)S(1)}, u32[]{:S(2)}, u32[]{:S(2)}) collective-permute-start(bf16[512,1024]{1,0:T(8,128)(2,1)S(1)} %fusion.20), channel_id=1, source_target_pairs={{0,2},{1,3},{2,0},{3,1},{4,6},{5,7},{6,4},{7,5},{8,10},{9,11},{10,... | collective-permute-start | bytes 3145736 | tf_op jit(solution)/shard_map/ppermute | solution.py:139
  53.6 48.1 %collective-permute-start.7 = (bf16[512,1024]{1,0:T(8,128)(2,1)}, bf16[512,1024]{1,0:T(8,128)(2,1)}, u32[]{:S(2)}, u32[]{:S(2)}) collective-permute-start(bf16[512,1024]{1,0:T(8,128)(2,1)} %param.19), channel_id=1, source_target_pairs={{0,1},{1,0},{2,3},{3,2},{4,5},{5,4},{6,7},{7,6},{8,9},{9,8},{10,11... | collective-permute-start | bytes 3145736 | tf_op jit(solution)/shard_map/ppermute | solution.py:139
  76.2 30.2 %collective-permute-start.12 = (bf16[512,1024]{1,0:T(8,128)(2,1)}, bf16[512,1024]{1,0:T(8,128)(2,1)}, u32[]{:S(2)}, u32[]{:S(2)}) collective-permute-start(bf16[512,1024]{1,0:T(8,128)(2,1)} %collective-permute-done.11), channel_id=1, source_target_pairs={{0,1},{1,0},{2,3},{3,2},{4,5},{5,4},{6,7},{7,6},{8,9},{9,8},{10,11... | collective-permute-start | bytes 3145736 | tf_op jit(solution)/shard_map/ppermute | solution.py:139
  100.0 25.0 %collective-permute-start.9 = (bf16[512,1024]{1,0:T(8,128)(2,1)}, bf16[512,1024]{1,0:T(8,128)(2,1)}, u32[]{:S(2)}, u32[]{:S(2)}) collective-permute-start(bf16[512,1024]{1,0:T(8,128)(2,1)} %multiply_convert_fusion), channel_id=1, source_target_pairs={{0,2},{1,3},{2,0},{3,1},{4,6},{5,7},{6,4},{7,5},{8,10},{9,11},{10,... | collective-permute-start | bytes 3145736 | tf_op jit(solution)/shard_map/ppermute | solution.py:139
  101.7 23.3 %collective-permute-start.6 = (bf16[512,1024]{1,0:T(8,128)(2,1)}, bf16[512,1024]{1,0:T(8,128)(2,1)}, u32[]{:S(2)}, u32[]{:S(2)}) collective-permute-start(bf16[512,1024]{1,0:T(8,128)(2,1)} %multiply_convert_fusion), channel_id=1, source_target_pairs={{0,1},{1,0},{2,3},{3,2},{4,5},{5,4},{6,7},{7,6},{8,9},{9,8},{10,11... | collective-permute-start | bytes 3145736 | tf_op jit(solution)/shard_map/ppermute | solution.py:139
  125.0 43.6 %collective-permute-start.10 = (bf16[512,1024]{1,0:T(8,128)(2,1)}, bf16[512,1024]{1,0:T(8,128)(2,1)S(1)}, u32[]{:S(2)}, u32[]{:S(2)}) collective-permute-start(bf16[512,1024]{1,0:T(8,128)(2,1)} %collective-permute-done.9), channel_id=1, source_target_pairs={{0,1},{1,0},{2,3},{3,2},{4,5},{5,4},{6,7},{7,6},{8,9},{9,8},{10,11... | collective-permute-start | bytes 3145736 | tf_op jit(solution)/shard_map/ppermute | solution.py:139
  168.1 118.7 %collective-permute-start.8 = (bf16[512,1024]{1,0:T(8,128)(2,1)}, bf16[512,1024]{1,0:T(8,128)(2,1)S(1)}, u32[]{:S(2)}, u32[]{:S(2)}) collective-permute-start(bf16[512,1024]{1,0:T(8,128)(2,1)} %dynamic-slice_bitcast_fusion.3), channel_id=1, source_target_pairs={{0,1},{1,0},{2,3},{3,2},{4,5},{5,4},{6,7},{7,6},{8,9},{9,8},{10,11... | collective-permute-start | bytes 3145736 | tf_op jit(solution)/shard_map/ppermute | solution.py:139
  210.2 46.3 %collective-permute-start.13 = (bf16[512,1024]{1,0:T(8,128)(2,1)S(1)}, bf16[512,1024]{1,0:T(8,128)(2,1)S(1)}, u32[]{:S(2)}, u32[]{:S(2)}) collective-permute-start(bf16[512,1024]{1,0:T(8,128)(2,1)S(1)} %dynamic-slice_bitcast_fusion.2), channel_id=1, source_target_pairs={{0,1},{1,0},{2,3},{3,2},{4,5},{5,4},{6,7},{7,6},{8,9},{9,8},{10,11... | collective-permute-start | bytes 3145736 | tf_op jit(solution)/shard_map/ppermute | solution.py:139
  214.1 16.2 %collective-permute-start.62 = (bf16[256,1152]{1,0:T(8,128)(2,1)S(1)}, bf16[256,1152]{1,0:T(8,128)(2,1)S(1)}, u32[]{:S(2)}, u32[]{:S(2)}) collective-permute-start(bf16[256,1152]{1,0:T(8,128)(2,1)S(1)} %fusion.40), channel_id=1, source_target_pairs={{0,4},{4,0},{8,12},{12,8},{16,20},{20,16},{24,28},{28,24},{1,5},{5... | collective-permute-start | bytes 1769480 | tf_op jit(solution)/shard_map/ppermute | solution.py:139
  215.9 26.6 %collective-permute-start.56 = (bf16[256,1152]{1,0:T(8,128)(2,1)S(1)}, bf16[256,1152]{1,0:T(8,128)(2,1)S(1)}, u32[]{:S(2)}, u32[]{:S(2)}) collective-permute-start(bf16[256,1152]{1,0:T(8,128)(2,1)S(1)} %fusion.39), channel_id=1, source_target_pairs={{0,4},{4,0},{8,12},{12,8},{16,20},{20,16},{24,28},{28,24},{1,5},{5... | collective-permute-start | bytes 1769480 | tf_op jit(solution)/shard_map/ppermute | solution.py:139
  230.4 14.1 %collective-permute-start.63 = (bf16[128,1152]{1,0:T(8,128)(2,1)S(1)}, bf16[128,1152]{1,0:T(8,128)(2,1)S(1)}, u32[]{:S(2)}, u32[]{:S(2)}) collective-permute-start(bf16[128,1152]{1,0:T(8,128)(2,1)S(1)} %fusion.50), channel_id=1, source_target_pairs={{0,8},{4,12},{8,0},{12,4},{16,24},{20,28},{24,16},{28,20},{1,9},{5... | collective-permute-start | bytes 884744 | tf_op jit(solution)/shard_map/ppermute | solution.py:139
  242.7 11.9 %collective-permute-start.57 = (bf16[128,1152]{1,0:T(8,128)(2,1)S(1)}, bf16[128,1152]{1,0:T(8,128)(2,1)S(1)}, u32[]{:S(2)}, u32[]{:S(2)}) collective-permute-start(bf16[128,1152]{1,0:T(8,128)(2,1)S(1)} %fusion.49), channel_id=1, source_target_pairs={{0,8},{4,12},{8,0},{12,4},{16,24},{20,28},{24,16},{28,20},{1,9},{5... | collective-permute-start | bytes 884744 | tf_op jit(solution)/shard_map/ppermute | solution.py:139
  244.6 11.9 %collective-permute-start.64 = (bf16[64,1152]{1,0:T(8,128)(2,1)S(1)}, bf16[64,1152]{1,0:T(8,128)(2,1)S(1)}, u32[]{:S(2)}, u32[]{:S(2)}) collective-permute-start(bf16[64,1152]{1,0:T(8,128)(2,1)S(1)} %fusion.66), channel_id=1, source_target_pairs={{0,16},{4,20},{8,24},{12,28},{16,0},{20,4},{24,8},{28,12},{1,17},{... | collective-permute-start | bytes 442376 | tf_op jit(solution)/shard_map/ppermute | solution.py:139
  257.1 16.3 %collective-permute-start.74 = (bf16[256,1152]{1,0:T(8,128)(2,1)S(1)}, bf16[256,1152]{1,0:T(8,128)(2,1)S(1)}, u32[]{:S(2)}, u32[]{:S(2)}) collective-permute-start(bf16[256,1152]{1,0:T(8,128)(2,1)S(1)} %fusion.42), channel_id=1, source_target_pairs={{0,4},{4,0},{8,12},{12,8},{16,20},{20,16},{24,28},{28,24},{1,5},{5... | collective-permute-start | bytes 1769480 | tf_op jit(solution)/shard_map/ppermute | solution.py:139
  263.4 24.0 %collective-permute-start.14 = (bf16[512,1024]{1,0:T(8,128)(2,1)S(1)}, bf16[512,1024]{1,0:T(8,128)(2,1)S(1)}, u32[]{:S(2)}, u32[]{:S(2)}) collective-permute-start(bf16[512,1024]{1,0:T(8,128)(2,1)S(1)} %fusion.16), channel_id=1, source_target_pairs={{0,2},{1,3},{2,0},{3,1},{4,6},{5,7},{6,4},{7,5},{8,10},{9,11},{10,... | collective-permute-start | bytes 3145736 | tf_op jit(solution)/shard_map/ppermute | solution.py:139
  265.1 18.4 %collective-permute-start.68 = (bf16[256,1152]{1,0:T(8,128)(2,1)S(1)}, bf16[256,1152]{1,0:T(8,128)(2,1)S(1)}, u32[]{:S(2)}, u32[]{:S(2)}) collective-permute-start(bf16[256,1152]{1,0:T(8,128)(2,1)S(1)} %fusion.41), channel_id=1, source_target_pairs={{0,4},{4,0},{8,12},{12,8},{16,20},{20,16},{24,28},{28,24},{1,5},{5... | collective-permute-start | bytes 1769480 | tf_op jit(solution)/shard_map/ppermute | solution.py:139
  273.6 12.7 %collective-permute-start.75 = (bf16[128,1152]{1,0:T(8,128)(2,1)S(1)}, bf16[128,1152]{1,0:T(8,128)(2,1)S(1)}, u32[]{:S(2)}, u32[]{:S(2)}) collective-permute-start(bf16[128,1152]{1,0:T(8,128)(2,1)S(1)} %fusion.52), channel_id=1, source_target_pairs={{0,8},{4,12},{8,0},{12,4},{16,24},{20,28},{24,16},{28,20},{1,9},{5... | collective-permute-start | bytes 884744 | tf_op jit(solution)/shard_map/ppermute | solution.py:139
  283.7 10.5 %collective-permute-start.69 = (bf16[128,1152]{1,0:T(8,128)(2,1)S(1)}, bf16[128,1152]{1,0:T(8,128)(2,1)S(1)}, u32[]{:S(2)}, u32[]{:S(2)}) collective-permute-start(bf16[128,1152]{1,0:T(8,128)(2,1)S(1)} %fusion.51), channel_id=1, source_target_pairs={{0,8},{4,12},{8,0},{12,4},{16,24},{20,28},{24,16},{28,20},{1,9},{5... | collective-permute-start | bytes 884744 | tf_op jit(solution)/shard_map/ppermute | solution.py:139
  290.6 23.1 %collective-permute-start.15 = (bf16[512,1024]{1,0:T(8,128)(2,1)S(1)}, bf16[512,1024]{1,0:T(8,128)(2,1)S(1)}, u32[]{:S(2)}, u32[]{:S(2)}) collective-permute-start(bf16[512,1024]{1,0:T(8,128)(2,1)S(1)} %get-tuple-element.71), channel_id=1, source_target_pairs={{0,2},{1,3},{2,0},{3,1},{4,6},{5,7},{6,4},{7,5},{8,10},{9,11},{10,... | collective-permute-start | bytes 3145736 | tf_op jit(solution)/shard_map/ppermute | solution.py:139
  294.3 19.5 %collective-permute-start.20 = (bf16[512,1024]{1,0:T(8,128)(2,1)S(1)}, bf16[512,1024]{1,0:T(8,128)(2,1)S(1)}, u32[]{:S(2)}, u32[]{:S(2)}) collective-permute-start(bf16[512,1024]{1,0:T(8,128)(2,1)S(1)} %get-tuple-element.71), channel_id=1, source_target_pairs={{0,1},{1,0},{2,3},{3,2},{4,5},{5,4},{6,7},{7,6},{8,9},{9,8},{10,11... | collective-permute-start | bytes 3145736 | tf_op jit(solution)/shard_map/ppermute | solution.py:139
  294.4 19.3 %collective-permute-start.70 = (bf16[64,1152]{1,0:T(8,128)(2,1)S(1)}, bf16[64,1152]{1,0:T(8,128)(2,1)S(1)}, u32[]{:S(2)}, u32[]{:S(2)}) collective-permute-start(bf16[64,1152]{1,0:T(8,128)(2,1)S(1)} %fusion.67), channel_id=1, source_target_pairs={{0,16},{4,20},{8,24},{12,28},{16,0},{20,4},{24,8},{28,12},{1,17},{... | collective-permute-start | bytes 442376 | tf_op jit(solution)/shard_map/ppermute | solution.py:139
  322.1 240.0 %collective-permute-start.18 = (bf16[512,1024]{1,0:T(8,128)(2,1)}, bf16[512,1024]{1,0:T(8,128)(2,1)}, u32[]{:S(2)}, u32[]{:S(2)}) collective-permute-start(bf16[512,1024]{1,0:T(8,128)(2,1)} %dynamic-slice_bitcast_fusion), channel_id=1, source_target_pairs={{0,1},{1,0},{2,3},{3,2},{4,5},{5,4},{6,7},{7,6},{8,9},{9,8},{10,11... | collective-permute-start | bytes 3145736 | tf_op jit(solution)/shard_map/ppermute | solution.py:139
  330.4 217.2 %collective-permute-start.22 = (bf16[512,1024]{1,0:T(8,128)(2,1)S(1)}, bf16[512,1024]{1,0:T(8,128)(2,1)S(1)}, u32[]{:S(2)}, u32[]{:S(2)}) collective-permute-start(bf16[512,1024]{1,0:T(8,128)(2,1)S(1)} %fusion.25), channel_id=1, source_target_pairs={{0,1},{1,0},{2,3},{3,2},{4,5},{5,4},{6,7},{7,6},{8,9},{9,8},{10,11... | collective-permute-start | bytes 3145736 | tf_op jit(solution)/shard_map/ppermute | solution.py:139
  340.2 40.2 %collective-permute-start.41 = (bf16[512,256]{1,0:T(8,128)(2,1)S(1)}, bf16[512,256]{1,0:T(8,128)(2,1)S(1)}, u32[]{:S(2)}, u32[]{:S(2)}) collective-permute-start(bf16[512,256]{1,0:T(8,128)(2,1)S(1)} %fusion.63), channel_id=1, source_target_pairs={{0,4},{4,0},{8,12},{12,8},{16,20},{20,16},{24,28},{28,24},{1,5},{5... | collective-permute-start | bytes 786440 | tf_op jit(solution)/shard_map/ppermute | solution.py:139
  343.1 16.1 %collective-permute-start.65 = (bf16[64,1152]{1,0:T(8,128)(2,1)S(1)}, bf16[64,1152]{1,0:T(8,128)(2,1)S(1)}, u32[]{:S(2)}, u32[]{:S(2)}) collective-permute-start(bf16[64,1152]{1,0:T(8,128)(2,1)S(1)} %fusion.59), channel_id=1, source_target_pairs={{0,16},{4,20},{8,24},{12,28},{16,0},{20,4},{24,8},{28,12},{1,17},{... | collective-permute-start | bytes 442376 | tf_op jit(solution)/shard_map/ppermute | solution.py:139
  357.6 25.1 %collective-permute-start.35 = (bf16[512,256]{1,0:T(8,128)(2,1)S(1)}, bf16[512,256]{1,0:T(8,128)(2,1)S(1)}, u32[]{:S(2)}, u32[]{:S(2)}) collective-permute-start(bf16[512,256]{1,0:T(8,128)(2,1)S(1)} %fusion.62), channel_id=1, source_target_pairs={{0,8},{4,12},{8,0},{12,4},{16,24},{20,28},{24,16},{28,20},{1,9},{5... | collective-permute-start | bytes 786440 | tf_op jit(solution)/shard_map/ppermute | solution.py:139
  382.7 96.5 %collective-permute-start.86 = (bf16[288,1024]{1,0:T(8,128)(2,1)S(1)}, bf16[288,1024]{1,0:T(8,128)(2,1)S(1)}, u32[]{:S(2)}, u32[]{:S(2)}) collective-permute-start(bf16[288,1024]{1,0:T(8,128)(2,1)S(1)} %fusion.44), channel_id=1, source_target_pairs={{0,4},{4,0},{8,12},{12,8},{16,20},{20,16},{24,28},{28,24},{1,5},{5... | collective-permute-start | bytes 1769480 | tf_op jit(solution)/shard_map/ppermute | solution.py:139
  388.1 34.8 %collective-permute-start.66 = (bf16[128,1152]{1,0:T(8,128)(2,1)S(1)}, bf16[128,1152]{1,0:T(8,128)(2,1)S(1)}, u32[]{:S(2)}, u32[]{:S(2)}) collective-permute-start(bf16[128,1152]{1,0:T(8,128)(2,1)S(1)} %maximum_select_fusion.29), channel_id=1, source_target_pairs={{0,8},{4,12},{8,0},{12,4},{16,24},{20,28},{24,16},{28,20},{1,9},{5... | collective-permute-start | bytes 884744 | tf_op jit(solution)/shard_map/ppermute | solution.py:139
  431.4 50.3 %collective-permute-start.80 = (bf16[288,1024]{1,0:T(8,128)(2,1)S(1)}, bf16[288,1024]{1,0:T(8,128)(2,1)S(1)}, u32[]{:S(2)}, u32[]{:S(2)}) collective-permute-start(bf16[288,1024]{1,0:T(8,128)(2,1)S(1)} %fusion.43), channel_id=1, source_target_pairs={{0,4},{4,0},{8,12},{12,8},{16,20},{20,16},{24,28},{28,24},{1,5},{5... | collective-permute-start | bytes 1769480 | tf_op jit(solution)/shard_map/ppermute | solution.py:139
  488.7 11.2 %collective-permute-start.81 = (bf16[144,1024]{1,0:T(8,128)(2,1)S(1)}, bf16[144,1024]{1,0:T(8,128)(2,1)S(1)}, u32[]{:S(2)}, u32[]{:S(2)}) collective-permute-start(bf16[144,1024]{1,0:T(8,128)(2,1)S(1)} %fusion.53), channel_id=1, source_target_pairs={{0,8},{4,12},{8,0},{12,4},{16,24},{20,28},{24,16},{28,20},{1,9},{5... | collective-permute-start | bytes 884744 | tf_op jit(solution)/shard_map/ppermute | solution.py:139
  501.7 22.5 %collective-permute-start.67 = (bf16[256,1152]{1,0:T(8,128)(2,1)S(1)}, bf16[256,1152]{1,0:T(8,128)(2,1)S(1)}, u32[]{:S(2)}, u32[]{:S(2)}) collective-permute-start(bf16[256,1152]{1,0:T(8,128)(2,1)S(1)} %maximum_select_fusion.15), channel_id=1, source_target_pairs={{0,4},{4,0},{8,12},{12,8},{16,20},{20,16},{24,28},{28,24},{1,5},{5... | collective-permute-start | bytes 1769480 | tf_op jit(solution)/shard_map/ppermute | solution.py:139
  510.5 14.2 %collective-permute-start.61 = (bf16[256,1152]{1,0:T(8,128)(2,1)S(1)}, bf16[256,1152]{1,0:T(8,128)(2,1)S(1)}, u32[]{:S(2)}, u32[]{:S(2)}) collective-permute-start(bf16[256,1152]{1,0:T(8,128)(2,1)S(1)} %maximum_select_fusion.14), channel_id=1, source_target_pairs={{0,4},{4,0},{8,12},{12,8},{16,20},{20,16},{24,28},{28,24},{1,5},{5... | collective-permute-start | bytes 1769480 | tf_op jit(solution)/shard_map/ppermute | solution.py:139
  520.9 16.6 %collective-permute-start.79 = (bf16[256,1152]{1,0:T(8,128)(2,1)S(1)}, bf16[256,1152]{1,0:T(8,128)(2,1)S(1)}, u32[]{:S(2)}, u32[]{:S(2)}) collective-permute-start(bf16[256,1152]{1,0:T(8,128)(2,1)S(1)} %maximum_select_fusion.17), channel_id=1, source_target_pairs={{0,4},{4,0},{8,12},{12,8},{16,20},{20,16},{24,28},{28,24},{1,5},{5... | collective-permute-start | bytes 1769480 | tf_op jit(solution)/shard_map/ppermute | solution.py:139
  524.2 45.9 %collective-permute-start.21 = (bf16[512,1024]{1,0:T(8,128)(2,1)S(1)}, bf16[512,1024]{1,0:T(8,128)(2,1)S(1)}, u32[]{:S(2)}, u32[]{:S(2)}) collective-permute-start(bf16[512,1024]{1,0:T(8,128)(2,1)S(1)} %fusion.24), channel_id=1, source_target_pairs={{0,1},{1,0},{2,3},{3,2},{4,5},{5,4},{6,7},{7,6},{8,9},{9,8},{10,11... | collective-permute-start | bytes 3145736 | tf_op jit(solution)/shard_map/ppermute | solution.py:139
  524.7 19.9 %collective-permute-start.73 = (bf16[256,1152]{1,0:T(8,128)(2,1)S(1)}, bf16[256,1152]{1,0:T(8,128)(2,1)S(1)}, u32[]{:S(2)}, u32[]{:S(2)}) collective-permute-start(bf16[256,1152]{1,0:T(8,128)(2,1)S(1)} %maximum_select_fusion.16), channel_id=1, source_target_pairs={{0,4},{4,0},{8,12},{12,8},{16,20},{20,16},{24,28},{28,24},{1,5},{5... | collective-permute-start | bytes 1769480 | tf_op jit(solution)/shard_map/ppermute | solution.py:139
  537.5 10.0 %collective-permute-start.89 = (bf16[72,1024]{1,0:T(8,128)(2,1)S(1)}, bf16[72,1024]{1,0:T(8,128)(2,1)S(1)}, u32[]{:S(2)}, u32[]{:S(2)}) collective-permute-start(bf16[72,1024]{1,0:T(8,128)(2,1)S(1)} %fusion.55), channel_id=1, source_target_pairs={{0,16},{4,20},{8,24},{12,28},{16,0},{20,4},{24,8},{28,12},{1,17},{... | collective-permute-start | bytes 442376 | tf_op jit(solution)/shard_map/ppermute | solution.py:139
  547.6 10.5 %collective-permute-start.90 = (bf16[144,1024]{1,0:T(8,128)(2,1)S(1)}, bf16[144,1024]{1,0:T(8,128)(2,1)S(1)}, u32[]{:S(2)}, u32[]{:S(2)}) collective-permute-start(bf16[144,1024]{1,0:T(8,128)(2,1)S(1)} %maximum_select_fusion.33), channel_id=1, source_target_pairs={{0,8},{4,12},{8,0},{12,4},{16,24},{20,28},{24,16},{28,20},{1,9},{5... | collective-permute-start | bytes 884744 | tf_op jit(solution)/shard_map/ppermute | solution.py:139
  548.0 22.1 %collective-permute-start.23 = (bf16[512,1024]{1,0:T(8,128)(2,1)S(1)}, bf16[512,1024]{1,0:T(8,128)(2,1)S(1)}, u32[]{:S(2)}, u32[]{:S(2)}) collective-permute-start(bf16[512,1024]{1,0:T(8,128)(2,1)S(1)} %fusion.18), channel_id=1, source_target_pairs={{0,2},{1,3},{2,0},{3,1},{4,6},{5,7},{6,4},{7,5},{8,10},{9,11},{10,... | collective-permute-start | bytes 3145736 | tf_op jit(solution)/shard_map/ppermute | solution.py:139
  552.5 11.3 %collective-permute-start.84 = (bf16[144,1024]{1,0:T(8,128)(2,1)S(1)}, bf16[144,1024]{1,0:T(8,128)(2,1)S(1)}, u32[]{:S(2)}, u32[]{:S(2)}) collective-permute-start(bf16[144,1024]{1,0:T(8,128)(2,1)S(1)} %maximum_select_fusion.32), channel_id=1, source_target_pairs={{0,8},{4,12},{8,0},{12,4},{16,24},{20,28},{24,16},{28,20},{1,9},{5... | collective-permute-start | bytes 884744 | tf_op jit(solution)/shard_map/ppermute | solution.py:139
  558.3 9.9 %collective-permute-start.91 = (bf16[288,1024]{1,0:T(8,128)(2,1)S(1)}, bf16[288,1024]{1,0:T(8,128)(2,1)S(1)}, u32[]{:S(2)}, u32[]{:S(2)}) collective-permute-start(bf16[288,1024]{1,0:T(8,128)(2,1)S(1)} %maximum_select_fusion.19), channel_id=1, source_target_pairs={{0,4},{4,0},{8,12},{12,8},{16,20},{20,16},{24,28},{28,24},{1,5},{5... | collective-permute-start | bytes 1769480 | tf_op jit(solution)/shard_map/ppermute | solution.py:139
  562.1 37.4 %collective-permute-start.17 = (bf16[512,1024]{1,0:T(8,128)(2,1)S(1)}, bf16[512,1024]{1,0:T(8,128)(2,1)S(1)}, u32[]{:S(2)}, u32[]{:S(2)}) collective-permute-start(bf16[512,1024]{1,0:T(8,128)(2,1)S(1)} %copy-done.28), channel_id=1, source_target_pairs={{0,1},{1,0},{2,3},{3,2},{4,5},{5,4},{6,7},{7,6},{8,9},{9,8},{10,11... | collective-permute-start | bytes 3145736 | tf_op jit(solution)/shard_map/ppermute | solution.py:139
  563.8 35.7 %collective-permute-start.19 = (bf16[512,1024]{1,0:T(8,128)(2,1)S(1)}, bf16[512,1024]{1,0:T(8,128)(2,1)S(1)}, u32[]{:S(2)}, u32[]{:S(2)}) collective-permute-start(bf16[512,1024]{1,0:T(8,128)(2,1)S(1)} %fusion.12), channel_id=1, source_target_pairs={{0,2},{1,3},{2,0},{3,1},{4,6},{5,7},{6,4},{7,5},{8,10},{9,11},{10,... | collective-permute-start | bytes 3145736 | tf_op jit(solution)/shard_map/ppermute | solution.py:139
  568.2 12.9 %collective-permute-start.85 = (bf16[288,1024]{1,0:T(8,128)(2,1)S(1)}, bf16[288,1024]{1,0:T(8,128)(2,1)S(1)}, u32[]{:S(2)}, u32[]{:S(2)}) collective-permute-start(bf16[288,1024]{1,0:T(8,128)(2,1)S(1)} %maximum_select_fusion.18), channel_id=1, source_target_pairs={{0,4},{4,0},{8,12},{12,8},{16,20},{20,16},{24,28},{28,24},{1,5},{5... | collective-permute-start | bytes 1769480 | tf_op jit(solution)/shard_map/ppermute | solution.py:139
  571.2 10.5 %collective-permute-start.24 = (f32[2,1024]{1,0:T(2,128)S(1)}, f32[2,1024]{1,0:T(2,128)S(1)}, u32[]{:S(2)}, u32[]{:S(2)}) collective-permute-start(f32[2,1024]{1,0:T(2,128)S(1)} %pad_maximum_fusion.7), channel_id=1, source_target_pairs={{0,1},{1,0},{2,3},{3,2},{4,5},{5,4},{6,7},{7,6},{8,9},{9,8},{10,11... | collective-permute-start | bytes 24584 | tf_op jit(solution)/shard_map/ppermute | solution.py:139
  (91 other events, 743.8 us)

commit v3 on v2

--- a/solution.py
+++ b/solution.py
@@ -147,11 +147,17 @@
         give = lax.dynamic_index_in_dim(two, 1 - side, 0, keepdims=False)
         return keep, give
 
-    def gather(own):
+    def gather_start(own):
         far = swap(own, "tensor", 2)
         near = swap(own, "tensor", 1)
-        far_near = swap(far, "tensor", 1)
-        return ordered(core, own, near), ordered(core, far, far_near)
+        return ordered(core, own, near), far
+
+    def gather_end(far):
+        return ordered(core, far, swap(far, "tensor", 1))
+
+    def gather(own):
+        mine, far = gather_start(own)
+        return mine, gather_end(far)
 
     def scatter(mine, other):
         keep, give = parted(core, other)
@@ -226,41 +232,37 @@
     inputs = tokens.astype(F32)
     scale_one = rms_scale(inputs)
     first_m, first_o = gather((inputs * scale_one * mixer_gain).astype(BF16))
-    cot_m, cot_o = gather(after(out_grad, first_o))
     kept_o, part_o = conv_forward(first_o)
     kept_m, part_m = conv_forward(first_m)
     middle = inputs + scatter(part_m, part_o)[0]
     scale_two = rms_scale(middle)
-    second_m, second_o = gather((middle * scale_two * mlp_gain).astype(BF16))
+    second_local = (middle * scale_two * mlp_gain).astype(BF16)
+    second_m, second_far = gather_start(second_local)
+    cot_m, cot_far = gather_start(after(out_grad, second_local))
     out_m, back_m, *w_grads_m = mlp(second_m, cot_m, gate_weight, up_weight, down_weight)
+    second_far, cot_far, out_m = lax.optimization_barrier((second_far, cot_far, out_m))
+    second_o, cot_o = gather_end(second_far), gather_end(cot_far)
     out_o, back_o, *w_grads_o = mlp(second_o, cot_o, gate_weight, up_weight, down_weight)
     second_grad, sent = scatter(back_m, back_o)
 
-    halves = []
-    for grad_m, grad_o in zip(w_grads_m, w_grads_o):
-        half = grad_m.shape[0] // 2
-        for rows in (slice(0, half), slice(half, None)):
-            halves.append(grad_m[rows].astype(F32) + grad_o[rows].astype(F32))
-    pieces = [reduce_dp(half) for half in halves[:2]]
-    pieces += [reduce_dp(after(half, sent)) for half in halves[2:4]]
+    gate_w, up_w, down_w = (m.astype(F32) + o.astype(F32) for m, o in zip(w_grads_m, w_grads_o))
+    gate_piece = reduce_dp(after(gate_w, sent), 0)
+    up_piece = reduce_dp(after(up_w, sent), 1)
 
     mlp_gain_part = jnp.sum(second_grad * middle * scale_two, axis=0)
     middle_grad = out_grad.astype(F32) + norm_back(second_grad, middle, scale_two, mlp_gain)
     branch_m, branch_o = gather(middle_grad.astype(BF16))
-    pieces += [reduce_dp(after(half, branch_o)) for half in halves[4:]]
-    sums = [spread_dp(after(piece, branch_o)) for piece in pieces]
-    gate_w_grad, up_w_grad, down_grad = (
-        jnp.concatenate(sums[k : k + 2]) for k in range(0, 6, 2)
-    )
+    down_grad = sum_dp(after(down_w, branch_o), 0)
+    gate_w_grad = spread_dp(after(gate_piece, branch_o), 0)
+    up_w_grad = spread_dp(after(up_piece, branch_o), 1)
     output = (middle + scatter(after(out_m, branch_o), after(out_o, branch_o))[0]).astype(BF16)
 
     out_w_grad = sum_dp(dot_rows(kept_m[5], branch_m) + dot_rows(kept_o[5], branch_o), 1)
     stream_grad_o, conv_grad_o, back_o = conv_backward(kept_o, branch_o)
     stream_grad_m, conv_grad_m, back_m = conv_backward(kept_m, branch_m)
     in_flat_grad = dot_rows(first_m, stream_grad_m) + dot_rows(first_o, stream_grad_o)
-    in_w_grad = jnp.stack(
-        [sum_dp(in_flat_grad[:, k * chans : (k + 1) * chans], k % 2) for k in range(3)]
-    )
+    in_flat_grad = sum_dp(in_flat_grad, 0)
+    in_w_grad = jnp.stack([in_flat_grad[:, k * chans : (k + 1) * chans] for k in range(3)])
     first_grad = scatter(back_m, back_o)[0]
     mixer_gain_part = jnp.sum(first_grad * inputs * scale_one, axis=0)
     input_grad = (middle_grad + norm_back(first_grad, inputs, scale_one, mixer_gain)).astype(BF16)

time: 613 us -> 538 us (0.88)
  starting transfers between devices: 121 us -> 65.1 us
  waiting for transfers between devices: 301 us -> 279 us
  Pallas kernels: 72.5 us -> 81.1 us
  other arithmetic: 66.8 us -> 60.6 us
    ppermute x92 -> x62, starting transfers between devices: 121 us -> 65.1 us  [swap(): return lax.ppermute(value, axis, [(i, i ^ bit) for i in range(size[axis])])]
    ppermute x92 -> x62, waiting for transfers between devices: 301 us -> 279 us  [swap(): return lax.ppermute(value, axis, [(i, i ^ bit) for i in range(size[axis])])]
    select_n x35 -> x15, other arithmetic: 28.1 us -> 17.6 us  [ordered(): jnp.where(side == 0, jnp.concatenate([own, other]), jnp.concatenate([othe...]
    convert_element_type x1 -> x5, other arithmetic: 1.1 us -> 10.3 us  [spread_dp(): return current.astype(F32)]
    pallas_call x2, Pallas kernels: 72.5 us -> 81.1 us  [mlp(): pl.pallas_call(mlp_kernel, grid=(rows // tile,), in_specs=[by_rows, by_ro...]
    concatenate x3 -> x0, other arithmetic: 7.69 us -> none  [body(): jnp.concatenate(sums[k:k + 2])]
  transfers between devices with their start and end apart: 92 -> 62, of which waited for: 55 -> 28; matrix products, arithmetic and copies ran while one was open for 13% -> 15% of each run, Pallas kernels for 12% -> 15%
where the time goes in v3:
time: 538 us; the launch traced here: 534 us
  waiting for transfers between devices  279 us (52%)
  Pallas kernels  81.1 us (15%)
  starting transfers between devices  65.1 us (12%)
  other arithmetic  60.6 us (11%)
  matrix products  27.9 us (5%)
  local copies, waits for them, and re-layouts  18.2 us (3%)
    ppermute x62, waiting for transfers between devices, swap(): return lax.ppermute(value, axis, [(i, i ^ bit) for i in range(size[axis])])  279 us
    pallas_call x2, Pallas kernels, mlp(): pl.pallas_call(mlp_kernel, grid=(rows // tile,), in_specs=[by_rows, by_ro...  81.1 us
    ppermute x62, starting transfers between devices, swap(): return lax.ppermute(value, axis, [(i, i ^ bit) for i in range(size[axis])])  65.1 us
    select_n x15, other arithmetic, ordered(): jnp.where(side == 0, jnp.concatenate([own, other]), jnp.concatenate([othe...  17.6 us
    dot_general x4, matrix products, dot_rows(): lax.dot_general(a, b, (((0,), (0,)), ((), ())), preferred_element_type=F32)  10.8 us
  transfers between devices with their start and end apart: 62, of which 28 were waited for; matrix products, arithmetic and copies ran while one was open for 15% of the time, Pallas kernels for 15%

profile of v3, /device:TPU:0, one launch (start us, length us, event | category | flops | bytes accessed | tf_op | source)
XLA Modules:
  0.0 533.9 jit_solution(8741582426934914252)
XLA Ops:
  3.9 3.0 collective-permute-start.2
  6.9 23.3 %collective-permute-done.2 = bf16[512,1024]{1,0:T(8,128)(2,1)} collective-permute-done((bf16[512,1024]{1,0:T(8,128)(2,1)S(1)}, bf16[512,1024]{1,0:T(8,128)(2,1)}, u32[]{:S(2)}, u32[]{:S(2)}) %collective-permute-start.2) | collective-permute-done | bytes 1048608 | tf_op jit(solution)/shard_map/ppermute | solution.py:139
  30.4 3.9 fusion.57
  34.5 5.3 fusion.56
  39.9 2.4 fusion.41
  51.7 23.7 %collective-permute-done.5 = bf16[512,1024]{1,0:T(8,128)(2,1)S(1)} collective-permute-done((bf16[512,1024]{1,0:T(8,128)(2,1)S(1)}, bf16[512,1024]{1,0:T(8,128)(2,1)S(1)}, u32[]{:S(2)}, u32[]{:S(2)}) %collective-permute-start.5) | collective-permute-done | bytes 1048608 | tf_op jit(solution)/shard_map/ppermute | solution.py:139
  79.2 2.3 maximum_select_fusion.5.second_ref
  81.6 2.3 maximum_select_fusion.6.cot_ref
  83.9 35.9 %shard_map.177 = (bf16[1024,1024]{1,0:T(8,128)(2,1)}, bf16[1024,1024]{1,0:T(8,128)(2,1)}, bf16[1024,1152]{1,0:T(8,128)(2,1)}, bf16[1024,1152]{1,0:T(8,128)(2,1)}, bf16[1152,1024]{1,0:T(8,128)(2,1)}) custom-call(bf16[1024,1024]{1,0:T(8,128)(2,1)} %maximum_select_fusion.5.second_ref, bf16[1024,1024]{1,0:T(8,128)(2,1)} %maximum_select_fusion.6.cot_ref, ...), custom_call_target="tpu_custom_call" | custom-call | flops 21743271936 | bytes 22544384 | tf_op jit(solution)/shard_map/pallas_call | solution.py:102
  119.8 5.6 %collective-permute-done.7 = bf16[512,1024]{1,0:T(8,128)(2,1)} collective-permute-done((bf16[512,1024]{1,0:T(8,128)(2,1)S(1)}, bf16[512,1024]{1,0:T(8,128)(2,1)}, u32[]{:S(2)}, u32[]{:S(2)}) %collective-permute-start.7) | collective-permute-done | bytes 1048608 | tf_op jit(solution)/shard_map/ppermute | solution.py:139
  128.4 4.9 maximum_select_fusion.7.second_ref
  133.2 4.7 maximum_select_fusion.8.cot_ref
  137.9 45.3 %shard_map.178 = (bf16[1024,1024]{1,0:T(8,128)(2,1)}, bf16[1024,1024]{1,0:T(8,128)(2,1)}, bf16[1024,1152]{1,0:T(8,128)(2,1)}, bf16[1024,1152]{1,0:T(8,128)(2,1)}, bf16[1152,1024]{1,0:T(8,128)(2,1)}) custom-call(bf16[1024,1024]{1,0:T(8,128)(2,1)} %maximum_select_fusion.7.second_ref, bf16[1024,1024]{1,0:T(8,128)(2,1)} %maximum_select_fusion.8.cot_ref, ...), custom_call_target="tpu_custom_call" | custom-call | flops 21743271936 | bytes 22544384 | tf_op jit(solution)/shard_map/pallas_call | solution.py:102
  184.7 4.0 convert_add_fusion.1
  188.8 2.1 fusion.19
  192.7 2.7 convert_add_fusion
  198.9 17.5 %collective-permute-done.14 = bf16[512,1024]{1,0:T(8,128)(2,1)S(1)} collective-permute-done((bf16[512,1024]{1,0:T(8,128)(2,1)S(1)}, bf16[512,1024]{1,0:T(8,128)(2,1)S(1)}, u32[]{:S(2)}, u32[]{:S(2)}) %collective-permute-start.14) | collective-permute-done | bytes 1048608 | tf_op jit(solution)/shard_map/ppermute | solution.py:139
  220.1 3.4 collective-permute-done.44
  225.9 2.7 collective-permute-start.51
  228.5 22.1 %collective-permute-done.45 = bf16[256,1152]{1,0:T(8,128)(2,1)S(1)} collective-permute-done((bf16[256,1152]{1,0:T(8,128)(2,1)S(1)}, bf16[256,1152]{1,0:T(8,128)(2,1)S(1)}, u32[]{:S(2)}, u32[]{:S(2)}) %collective-permute-start.45) | collective-permute-done | bytes 589856 | tf_op jit(solution)/shard_map/ppermute | solution.py:139
  250.8 9.6 %collective-permute-done.51 = bf16[256,1152]{1,0:T(8,128)(2,1)S(1)} collective-permute-done((bf16[256,1152]{1,0:T(8,128)(2,1)S(1)}, bf16[256,1152]{1,0:T(8,128)(2,1)S(1)}, u32[]{:S(2)}, u32[]{:S(2)}) %collective-permute-start.51) | collective-permute-done | bytes 589856 | tf_op jit(solution)/shard_map/ppermute | solution.py:139
  262.2 4.1 collective-permute-done.46
  291.6 3.7 fusion.45
  295.3 4.5 convolution_add_fusion
  303.4 3.4 collective-permute-start.39
  306.9 2.8 collective-permute-start.37
  309.7 3.0 collective-permute-done.39
  315.6 2.2 collective-permute-done.40
  318.5 15.9 %collective-permute-done.41 = bf16[32,1024]{1,0:T(8,128)(2,1)S(1)} collective-permute-done((bf16[32,1024]{1,0:T(8,128)(2,1)S(1)}, bf16[32,1024]{1,0:T(8,128)(2,1)S(1)}, u32[]{:S(2)}, u32[]{:S(2)}) %collective-permute-start.41) | collective-permute-done | bytes 65568 | tf_op jit(solution)/shard_map/ppermute | solution.py:139
  334.5 3.0 collective-permute-start.42
  337.6 29.7 %collective-permute-done.42 = bf16[64,1024]{1,0:T(8,128)(2,1)S(1)} collective-permute-done((bf16[64,1024]{1,0:T(8,128)(2,1)S(1)}, bf16[64,1024]{1,0:T(8,128)(2,1)S(1)}, u32[]{:S(2)}, u32[]{:S(2)}) %collective-permute-start.42) | collective-permute-done | bytes 131104 | tf_op jit(solution)/shard_map/ppermute | solution.py:139
  371.9 13.5 %collective-permute-done.48 = bf16[256,1152]{1,0:T(8,128)(2,1)S(1)} collective-permute-done((bf16[256,1152]{1,0:T(8,128)(2,1)S(1)}, bf16[256,1152]{1,0:T(8,128)(2,1)S(1)}, u32[]{:S(2)}, u32[]{:S(2)}) %collective-permute-start.48) | collective-permute-done | bytes 589856 | tf_op jit(solution)/shard_map/ppermute | solution.py:139
  385.8 5.2 collective-permute-done.43
  392.1 5.7 %collective-permute-done.30 = bf16[256,768]{1,0:T(8,128)(2,1)S(1)} collective-permute-done((bf16[256,768]{1,0:T(8,128)(2,1)S(1)}, bf16[256,768]{1,0:T(8,128)(2,1)S(1)}, u32[]{:S(2)}, u32[]{:S(2)}) %collective-permute-start.30) | collective-permute-done | bytes 393248 | tf_op jit(solution)/shard_map/ppermute | solution.py:139
  399.2 9.3 %collective-permute-done.31 = bf16[128,768]{1,0:T(8,128)(2,1)S(1)} collective-permute-done((bf16[128,768]{1,0:T(8,128)(2,1)S(1)}, bf16[128,768]{1,0:T(8,128)(2,1)S(1)}, u32[]{:S(2)}, u32[]{:S(2)}) %collective-permute-start.31) | collective-permute-done | bytes 196640 | tf_op jit(solution)/shard_map/ppermute | solution.py:139
  408.5 2.5 collective-permute-start.32
  412.7 12.7 %collective-permute-done.32 = bf16[128,768]{1,0:T(8,128)(2,1)S(1)} collective-permute-done((bf16[128,768]{1,0:T(8,128)(2,1)S(1)}, bf16[128,768]{1,0:T(8,128)(2,1)S(1)}, u32[]{:S(2)}, u32[]{:S(2)}) %collective-permute-start.32) | collective-permute-done | bytes 196640 | tf_op jit(solution)/shard_map/ppermute | solution.py:139
  426.0 3.5 collective-permute-start.33
  431.4 6.5 %collective-permute-done.33 = bf16[256,768]{1,0:T(8,128)(2,1)S(1)} collective-permute-done((bf16[256,768]{1,0:T(8,128)(2,1)S(1)}, bf16[256,768]{1,0:T(8,128)(2,1)S(1)}, u32[]{:S(2)}, u32[]{:S(2)}) %collective-permute-start.33) | collective-permute-done | bytes 393248 | tf_op jit(solution)/shard_map/ppermute | solution.py:139
  441.6 2.8 fusion.2
  444.5 7.0 %collective-permute-done.23 = bf16[512,1024]{1,0:T(8,128)(2,1)S(1)} collective-permute-done((bf16[512,1024]{1,0:T(8,128)(2,1)S(1)}, bf16[512,1024]{1,0:T(8,128)(2,1)S(1)}, u32[]{:S(2)}, u32[]{:S(2)}) %collective-permute-start.23) | collective-permute-done | bytes 1048608 | tf_op jit(solution)/shard_map/ppermute | solution.py:139
  454.1 15.4 %collective-permute-done.58 = bf16[144,1024]{1,0:T(8,128)(2,1)S(1)} collective-permute-done((bf16[144,1024]{1,0:T(8,128)(2,1)S(1)}, bf16[144,1024]{1,0:T(8,128)(2,1)S(1)}, u32[]{:S(2)}, u32[]{:S(2)}) %collective-permute-start.58) | collective-permute-done | bytes 294944 | tf_op jit(solution)/shard_map/ppermute | solution.py:139
  470.8 3.4 collective-permute-start.59
  475.8 2.8 fusion.3
  480.3 7.5 %collective-permute-done.59 = bf16[144,1024]{1,0:T(8,128)(2,1)S(1)} collective-permute-done((bf16[144,1024]{1,0:T(8,128)(2,1)S(1)}, bf16[144,1024]{1,0:T(8,128)(2,1)S(1)}, u32[]{:S(2)}, u32[]{:S(2)}) %collective-permute-start.59) | collective-permute-done | bytes 294944 | tf_op jit(solution)/shard_map/ppermute | solution.py:139
  491.8 11.3 %collective-permute-done.27 = f32[2,1024]{1,0:T(2,128)S(1)} collective-permute-done((f32[2,1024]{1,0:T(2,128)S(1)}, f32[2,1024]{1,0:T(2,128)S(1)}, u32[]{:S(2)}, u32[]{:S(2)}) %collective-permute-start.27) | collective-permute-done | bytes 8224 | tf_op jit(solution)/shard_map/ppermute | solution.py:139
  510.8 19.6 %collective-permute-done.61 = bf16[576,1024]{1,0:T(8,128)(2,1)S(1)} collective-permute-done((bf16[576,1024]{1,0:T(8,128)(2,1)S(1)}, bf16[576,1024]{1,0:T(8,128)(2,1)S(1)}, u32[]{:S(2)}, u32[]{:S(2)}) %collective-permute-start.61) | collective-permute-done | bytes 1179680 | tf_op jit(solution)/shard_map/ppermute | solution.py:139
  530.4 3.2 fusion.4
  (268 shorter events, 101.1 us)
Async XLA Ops:
  3.9 26.3 %collective-permute-start.2 = (bf16[512,1024]{1,0:T(8,128)(2,1)S(1)}, bf16[512,1024]{1,0:T(8,128)(2,1)}, u32[]{:S(2)}, u32[]{:S(2)}) collective-permute-start(bf16[512,1024]{1,0:T(8,128)(2,1)S(1)} %fusion.5), channel_id=1, source_target_pairs={{0,2},{1,3},{2,0},{3,1},{4,6},{5,7},{6,4},{7,5},{8,10},{9,11},{10,... | collective-permute-start | bytes 3145736 | tf_op jit(solution)/shard_map/ppermute | solution.py:139
  6.9 23.4 %collective-permute-start = (bf16[512,1024]{1,0:T(8,128)(2,1)S(1)}, bf16[512,1024]{1,0:T(8,128)(2,1)}, u32[]{:S(2)}, u32[]{:S(2)}) collective-permute-start(bf16[512,1024]{1,0:T(8,128)(2,1)S(1)} %fusion.5), channel_id=1, source_target_pairs={{0,1},{1,0},{2,3},{3,2},{4,5},{5,4},{6,7},{7,6},{8,9},{9,8},{10,11... | collective-permute-start | bytes 3145736 | tf_op jit(solution)/shard_map/ppermute | solution.py:139
  49.9 25.5 %collective-permute-start.5 = (bf16[512,1024]{1,0:T(8,128)(2,1)S(1)}, bf16[512,1024]{1,0:T(8,128)(2,1)S(1)}, u32[]{:S(2)}, u32[]{:S(2)}) collective-permute-start(bf16[512,1024]{1,0:T(8,128)(2,1)S(1)} %fusion.23), channel_id=1, source_target_pairs={{0,2},{1,3},{2,0},{3,1},{4,6},{5,7},{6,4},{7,5},{8,10},{9,11},{10,... | collective-permute-start | bytes 3145736 | tf_op jit(solution)/shard_map/ppermute | solution.py:139
  77.2 42.5 %collective-permute-start.6 = (bf16[512,1024]{1,0:T(8,128)(2,1)S(1)}, bf16[512,1024]{1,0:T(8,128)(2,1)}, u32[]{:S(2)}, u32[]{:S(2)}) collective-permute-start(bf16[512,1024]{1,0:T(8,128)(2,1)S(1)} %multiply_convert_fusion), channel_id=1, source_target_pairs={{0,2},{1,3},{2,0},{3,1},{4,6},{5,7},{6,4},{7,5},{8,10},{9,11},{10,... | collective-permute-start | bytes 3145736 | tf_op jit(solution)/shard_map/ppermute | solution.py:139
  79.0 46.4 %collective-permute-start.7 = (bf16[512,1024]{1,0:T(8,128)(2,1)S(1)}, bf16[512,1024]{1,0:T(8,128)(2,1)}, u32[]{:S(2)}, u32[]{:S(2)}) collective-permute-start(bf16[512,1024]{1,0:T(8,128)(2,1)S(1)} %copy-done.16), channel_id=1, source_target_pairs={{0,2},{1,3},{2,0},{3,1},{4,6},{5,7},{6,4},{7,5},{8,10},{9,11},{10,... | collective-permute-start | bytes 3145736 | tf_op jit(solution)/shard_map/ppermute | solution.py:139
  125.4 7.9 %collective-permute-start.12 = (bf16[512,1024]{1,0:T(8,128)(2,1)}, bf16[512,1024]{1,0:T(8,128)(2,1)}, u32[]{:S(2)}, u32[]{:S(2)}) collective-permute-start(bf16[512,1024]{1,0:T(8,128)(2,1)} %collective-permute-done.7), channel_id=1, source_target_pairs={{0,1},{1,0},{2,3},{3,2},{4,5},{5,4},{6,7},{7,6},{8,9},{9,8},{10,11... | collective-permute-start | bytes 3145736 | tf_op jit(solution)/shard_map/ppermute | solution.py:139
  127.2 71.7 %collective-permute-start.10 = (bf16[512,1024]{1,0:T(8,128)(2,1)S(1)}, bf16[512,1024]{1,0:T(8,128)(2,1)S(1)}, u32[]{:S(2)}, u32[]{:S(2)}) collective-permute-start(bf16[512,1024]{1,0:T(8,128)(2,1)S(1)} %dynamic-slice_bitcast_fusion.3), channel_id=1, source_target_pairs={{0,1},{1,0},{2,3},{3,2},{4,5},{5,4},{6,7},{7,6},{8,9},{9,8},{10,11... | collective-permute-start | bytes 3145736 | tf_op jit(solution)/shard_map/ppermute | solution.py:139
  190.9 25.5 %collective-permute-start.14 = (bf16[512,1024]{1,0:T(8,128)(2,1)S(1)}, bf16[512,1024]{1,0:T(8,128)(2,1)S(1)}, u32[]{:S(2)}, u32[]{:S(2)}) collective-permute-start(bf16[512,1024]{1,0:T(8,128)(2,1)S(1)} %fusion.19), channel_id=1, source_target_pairs={{0,2},{1,3},{2,0},{3,1},{4,6},{5,7},{6,4},{7,5},{8,10},{9,11},{10,... | collective-permute-start | bytes 3145736 | tf_op jit(solution)/shard_map/ppermute | solution.py:139
  195.5 28.0 %collective-permute-start.44 = (bf16[512,1152]{1,0:T(8,128)(2,1)S(1)}, bf16[512,1152]{1,0:T(8,128)(2,1)S(1)}, u32[]{:S(2)}, u32[]{:S(2)}) collective-permute-start(bf16[512,1152]{1,0:T(8,128)(2,1)S(1)} %fusion.26), channel_id=1, source_target_pairs={{0,4},{4,0},{8,12},{12,8},{16,20},{20,16},{24,28},{28,24},{1,5},{5... | collective-permute-start | bytes 3538952 | tf_op jit(solution)/shard_map/ppermute | solution.py:139
  197.2 28.3 %collective-permute-start.50 = (bf16[512,1152]{1,0:T(8,128)(2,1)S(1)}, bf16[512,1152]{1,0:T(8,128)(2,1)S(1)}, u32[]{:S(2)}, u32[]{:S(2)}) collective-permute-start(bf16[512,1152]{1,0:T(8,128)(2,1)S(1)} %fusion.27), channel_id=1, source_target_pairs={{0,8},{4,12},{8,0},{12,4},{16,24},{20,28},{24,16},{28,20},{1,9},{5... | collective-permute-start | bytes 3538952 | tf_op jit(solution)/shard_map/ppermute | solution.py:139
  218.3 48.1 %collective-permute-start.15 = (bf16[512,1024]{1,0:T(8,128)(2,1)S(1)}, bf16[512,1024]{1,0:T(8,128)(2,1)S(1)}, u32[]{:S(2)}, u32[]{:S(2)}) collective-permute-start(bf16[512,1024]{1,0:T(8,128)(2,1)S(1)} %get-tuple-element.67), channel_id=1, source_target_pairs={{0,2},{1,3},{2,0},{3,1},{4,6},{5,7},{6,4},{7,5},{8,10},{9,11},{10,... | collective-permute-start | bytes 3145736 | tf_op jit(solution)/shard_map/ppermute | solution.py:139
  220.1 47.4 %collective-permute-start.20 = (bf16[512,1024]{1,0:T(8,128)(2,1)S(1)}, bf16[512,1024]{1,0:T(8,128)(2,1)S(1)}, u32[]{:S(2)}, u32[]{:S(2)}) collective-permute-start(bf16[512,1024]{1,0:T(8,128)(2,1)S(1)} %get-tuple-element.67), channel_id=1, source_target_pairs={{0,1},{1,0},{2,3},{3,2},{4,5},{5,4},{6,7},{7,6},{8,9},{9,8},{10,11... | collective-permute-start | bytes 3145736 | tf_op jit(solution)/shard_map/ppermute | solution.py:139
  223.9 26.7 %collective-permute-start.45 = (bf16[256,1152]{1,0:T(8,128)(2,1)S(1)}, bf16[256,1152]{1,0:T(8,128)(2,1)S(1)}, u32[]{:S(2)}, u32[]{:S(2)}) collective-permute-start(bf16[256,1152]{1,0:T(8,128)(2,1)S(1)} %fusion.47), channel_id=1, source_target_pairs={{0,8},{4,12},{8,0},{12,4},{16,24},{20,28},{24,16},{28,20},{1,9},{5... | collective-permute-start | bytes 1769480 | tf_op jit(solution)/shard_map/ppermute | solution.py:139
  225.9 34.6 %collective-permute-start.51 = (bf16[256,1152]{1,0:T(8,128)(2,1)S(1)}, bf16[256,1152]{1,0:T(8,128)(2,1)S(1)}, u32[]{:S(2)}, u32[]{:S(2)}) collective-permute-start(bf16[256,1152]{1,0:T(8,128)(2,1)S(1)} %fusion.48), channel_id=1, source_target_pairs={{0,16},{4,20},{8,24},{12,28},{16,0},{20,4},{24,8},{28,12},{1,17},{... | collective-permute-start | bytes 1769480 | tf_op jit(solution)/shard_map/ppermute | solution.py:139
  250.8 15.6 %collective-permute-start.46 = (bf16[128,1152]{1,0:T(8,128)(2,1)S(1)}, bf16[128,1152]{1,0:T(8,128)(2,1)S(1)}, u32[]{:S(2)}, u32[]{:S(2)}) collective-permute-start(bf16[128,1152]{1,0:T(8,128)(2,1)S(1)} %fusion.60), channel_id=1, source_target_pairs={{0,16},{4,20},{8,24},{12,28},{16,0},{20,4},{24,8},{28,12},{1,17},{... | collective-permute-start | bytes 884744 | tf_op jit(solution)/shard_map/ppermute | solution.py:139
  260.6 6.8 %collective-permute-start.52 = (bf16[128,1152]{1,0:T(8,128)(2,1)S(1)}, bf16[128,1152]{1,0:T(8,128)(2,1)S(1)}, u32[]{:S(2)}, u32[]{:S(2)}) collective-permute-start(bf16[128,1152]{1,0:T(8,128)(2,1)S(1)} %fusion.61), channel_id=1, source_target_pairs={{0,4},{4,0},{8,12},{12,8},{16,20},{20,16},{24,28},{28,24},{1,5},{5... | collective-permute-start | bytes 884744 | tf_op jit(solution)/shard_map/ppermute | solution.py:139
  276.8 149.1 %collective-permute-start.18 = (bf16[512,1024]{1,0:T(8,128)(2,1)}, bf16[512,1024]{1,0:T(8,128)(2,1)}, u32[]{:S(2)}, u32[]{:S(2)}) collective-permute-start(bf16[512,1024]{1,0:T(8,128)(2,1)} %dynamic-slice_bitcast_fusion), channel_id=1, source_target_pairs={{0,1},{1,0},{2,3},{3,2},{4,5},{5,4},{6,7},{7,6},{8,9},{9,8},{10,11... | collective-permute-start | bytes 3145736 | tf_op jit(solution)/shard_map/ppermute | solution.py:139
  285.8 122.7 %collective-permute-start.22 = (bf16[512,1024]{1,0:T(8,128)(2,1)}, bf16[512,1024]{1,0:T(8,128)(2,1)}, u32[]{:S(2)}, u32[]{:S(2)}) collective-permute-start(bf16[512,1024]{1,0:T(8,128)(2,1)} %fusion.32), channel_id=1, source_target_pairs={{0,1},{1,0},{2,3},{3,2},{4,5},{5,4},{6,7},{7,6},{8,9},{9,8},{10,11... | collective-permute-start | bytes 3145736 | tf_op jit(solution)/shard_map/ppermute | solution.py:139
  286.3 16.2 %collective-permute-start.35 = (f32[3,256]{1,0:T(4,128)S(1)}, f32[3,256]{1,0:T(4,128)S(1)}, u32[]{:S(2)}, u32[]{:S(2)}) collective-permute-start(f32[3,256]{1,0:T(4,128)S(1)} %maximum_add_fusion), channel_id=1, source_target_pairs={{0,4},{4,0},{8,12},{12,8},{16,20},{20,16},{24,28},{28,24},{1,5},{5... | collective-permute-start | bytes 9224 | tf_op jit(solution)/shard_map/ppermute | solution.py:139
  288.7 14.6 %collective-permute-start.38 = (bf16[128,1024]{1,0:T(8,128)(2,1)S(1)}, bf16[128,1024]{1,0:T(8,128)(2,1)S(1)}, u32[]{:S(2)}, u32[]{:S(2)}) collective-permute-start(bf16[128,1024]{1,0:T(8,128)(2,1)S(1)} %fusion.63), channel_id=1, source_target_pairs={{0,8},{4,12},{8,0},{12,4},{16,24},{20,28},{24,16},{28,20},{1,9},{5... | collective-permute-start | bytes 786440 | tf_op jit(solution)/shard_map/ppermute | solution.py:139
  301.0 16.9 %collective-permute-start.53 = (bf16[128,1152]{1,0:T(8,128)(2,1)S(1)}, bf16[128,1152]{1,0:T(8,128)(2,1)S(1)}, u32[]{:S(2)}, u32[]{:S(2)}) collective-permute-start(bf16[128,1152]{1,0:T(8,128)(2,1)S(1)} %fusion.51), channel_id=1, source_target_pairs={{0,4},{4,0},{8,12},{12,8},{16,20},{20,16},{24,28},{28,24},{1,5},{5... | collective-permute-start | bytes 884744 | tf_op jit(solution)/shard_map/ppermute | solution.py:139
  303.4 9.3 %collective-permute-start.39 = (bf16[64,1024]{1,0:T(8,128)(2,1)S(1)}, bf16[64,1024]{1,0:T(8,128)(2,1)S(1)}, u32[]{:S(2)}, u32[]{:S(2)}) collective-permute-start(bf16[64,1024]{1,0:T(8,128)(2,1)S(1)} %fusion.65), channel_id=1, source_target_pairs={{0,16},{4,20},{8,24},{12,28},{16,0},{20,4},{24,8},{28,12},{1,17},{... | collective-permute-start | bytes 393224 | tf_op jit(solution)/shard_map/ppermute | solution.py:139
  313.5 55.6 %collective-permute-start.29 = (bf16[512,768]{1,0:T(8,128)(2,1)S(1)}, bf16[512,768]{1,0:T(8,128)(2,1)S(1)}, u32[]{:S(2)}, u32[]{:S(2)}) collective-permute-start(bf16[512,768]{1,0:T(8,128)(2,1)S(1)} %fusion.43), channel_id=1, source_target_pairs={{0,4},{4,0},{8,12},{12,8},{16,20},{20,16},{24,28},{28,24},{1,5},{5... | collective-permute-start | bytes 2359304 | tf_op jit(solution)/shard_map/ppermute | solution.py:139
  317.8 16.7 %collective-permute-start.47 = (bf16[128,1152]{1,0:T(8,128)(2,1)S(1)}, bf16[128,1152]{1,0:T(8,128)(2,1)S(1)}, u32[]{:S(2)}, u32[]{:S(2)}) collective-permute-start(bf16[128,1152]{1,0:T(8,128)(2,1)S(1)} %fusion.52), channel_id=1, source_target_pairs={{0,16},{4,20},{8,24},{12,28},{16,0},{20,4},{24,8},{28,12},{1,17},{... | collective-permute-start | bytes 884744 | tf_op jit(solution)/shard_map/ppermute | solution.py:139
  317.9 16.5 %collective-permute-start.41 = (bf16[32,1024]{1,0:T(8,128)(2,1)S(1)}, bf16[32,1024]{1,0:T(8,128)(2,1)S(1)}, u32[]{:S(2)}, u32[]{:S(2)}) collective-permute-start(bf16[32,1024]{1,0:T(8,128)(2,1)S(1)} %fusion.66), channel_id=1, source_target_pairs={{0,4},{4,0},{8,12},{12,8},{16,20},{20,16},{24,28},{28,24},{1,5},{5... | collective-permute-start | bytes 196616 | tf_op jit(solution)/shard_map/ppermute | solution.py:139
  334.5 34.9 %collective-permute-start.54 = (bf16[256,1152]{1,0:T(8,128)(2,1)S(1)}, bf16[256,1152]{1,0:T(8,128)(2,1)S(1)}, u32[]{:S(2)}, u32[]{:S(2)}) collective-permute-start(bf16[256,1152]{1,0:T(8,128)(2,1)S(1)} %maximum_select_fusion.17), channel_id=1, source_target_pairs={{0,16},{4,20},{8,24},{12,28},{16,0},{20,4},{24,8},{28,12},{1,17},{... | collective-permute-start | bytes 1769480 | tf_op jit(solution)/shard_map/ppermute | solution.py:139
  334.5 32.8 %collective-permute-start.42 = (bf16[64,1024]{1,0:T(8,128)(2,1)S(1)}, bf16[64,1024]{1,0:T(8,128)(2,1)S(1)}, u32[]{:S(2)}, u32[]{:S(2)}) collective-permute-start(bf16[64,1024]{1,0:T(8,128)(2,1)S(1)} %maximum_select_fusion.28), channel_id=1, source_target_pairs={{0,16},{4,20},{8,24},{12,28},{16,0},{20,4},{24,8},{28,12},{1,17},{... | collective-permute-start | bytes 393224 | tf_op jit(solution)/shard_map/ppermute | solution.py:139
  367.3 31.0 %collective-permute-start.56 = (bf16[576,1024]{1,0:T(8,128)(2,1)S(1)}, bf16[576,1024]{1,0:T(8,128)(2,1)S(1)}, u32[]{:S(2)}, u32[]{:S(2)}) collective-permute-start(bf16[576,1024]{1,0:T(8,128)(2,1)S(1)} %fusion.28), channel_id=1, source_target_pairs={{0,4},{4,0},{8,12},{12,8},{16,20},{20,16},{24,28},{28,24},{1,5},{5... | collective-permute-start | bytes 3538952 | tf_op jit(solution)/shard_map/ppermute | solution.py:139
  369.0 16.3 %collective-permute-start.48 = (bf16[256,1152]{1,0:T(8,128)(2,1)S(1)}, bf16[256,1152]{1,0:T(8,128)(2,1)S(1)}, u32[]{:S(2)}, u32[]{:S(2)}) collective-permute-start(bf16[256,1152]{1,0:T(8,128)(2,1)S(1)} %maximum_select_fusion.16), channel_id=1, source_target_pairs={{0,8},{4,12},{8,0},{12,4},{16,24},{20,28},{24,16},{28,20},{1,9},{5... | collective-permute-start | bytes 1769480 | tf_op jit(solution)/shard_map/ppermute | solution.py:139
  369.4 21.6 %collective-permute-start.43 = (bf16[128,1024]{1,0:T(8,128)(2,1)S(1)}, bf16[128,1024]{1,0:T(8,128)(2,1)S(1)}, u32[]{:S(2)}, u32[]{:S(2)}) collective-permute-start(bf16[128,1024]{1,0:T(8,128)(2,1)S(1)} %maximum_select_fusion.27), channel_id=1, source_target_pairs={{0,8},{4,12},{8,0},{12,4},{16,24},{20,28},{24,16},{28,20},{1,9},{5... | collective-permute-start | bytes 786440 | tf_op jit(solution)/shard_map/ppermute | solution.py:139
  385.4 12.4 %collective-permute-start.30 = (bf16[256,768]{1,0:T(8,128)(2,1)S(1)}, bf16[256,768]{1,0:T(8,128)(2,1)S(1)}, u32[]{:S(2)}, u32[]{:S(2)}) collective-permute-start(bf16[256,768]{1,0:T(8,128)(2,1)S(1)} %fusion.54), channel_id=1, source_target_pairs={{0,8},{4,12},{8,0},{12,4},{16,24},{20,28},{24,16},{28,20},{1,9},{5... | collective-permute-start | bytes 1179656 | tf_op jit(solution)/shard_map/ppermute | solution.py:139
  391.0 53.4 %collective-permute-start.21 = (bf16[512,1024]{1,0:T(8,128)(2,1)}, bf16[512,1024]{1,0:T(8,128)(2,1)S(1)}, u32[]{:S(2)}, u32[]{:S(2)}) collective-permute-start(bf16[512,1024]{1,0:T(8,128)(2,1)} %fusion.31), channel_id=1, source_target_pairs={{0,1},{1,0},{2,3},{3,2},{4,5},{5,4},{6,7},{7,6},{8,9},{9,8},{10,11... | collective-permute-start | bytes 3145736 | tf_op jit(solution)/shard_map/ppermute | solution.py:139
  397.8 42.2 %collective-permute-start.49 = (bf16[512,1152]{1,0:T(8,128)(2,1)S(1)}, bf16[512,1152]{1,0:T(8,128)(2,1)S(1)}, u32[]{:S(2)}, u32[]{:S(2)}) collective-permute-start(bf16[512,1152]{1,0:T(8,128)(2,1)S(1)} %maximum_select_fusion.12), channel_id=1, source_target_pairs={{0,4},{4,0},{8,12},{12,8},{16,20},{20,16},{24,28},{28,24},{1,5},{5... | collective-permute-start | bytes 3538952 | tf_op jit(solution)/shard_map/ppermute | solution.py:139
  398.3 10.2 %collective-permute-start.31 = (bf16[128,768]{1,0:T(8,128)(2,1)S(1)}, bf16[128,768]{1,0:T(8,128)(2,1)S(1)}, u32[]{:S(2)}, u32[]{:S(2)}) collective-permute-start(bf16[128,768]{1,0:T(8,128)(2,1)S(1)} %fusion.64), channel_id=1, source_target_pairs={{0,16},{4,20},{8,24},{12,28},{16,0},{20,4},{24,8},{28,12},{1,17},{... | collective-permute-start | bytes 589832 | tf_op jit(solution)/shard_map/ppermute | solution.py:139
  408.5 22.6 %collective-permute-start.57 = (bf16[288,1024]{1,0:T(8,128)(2,1)S(1)}, bf16[288,1024]{1,0:T(8,128)(2,1)S(1)}, u32[]{:S(2)}, u32[]{:S(2)}) collective-permute-start(bf16[288,1024]{1,0:T(8,128)(2,1)S(1)} %fusion.49), channel_id=1, source_target_pairs={{0,8},{4,12},{8,0},{12,4},{16,24},{20,28},{24,16},{28,20},{1,9},{5... | collective-permute-start | bytes 1769480 | tf_op jit(solution)/shard_map/ppermute | solution.py:139
  408.5 16.9 %collective-permute-start.32 = (bf16[128,768]{1,0:T(8,128)(2,1)S(1)}, bf16[128,768]{1,0:T(8,128)(2,1)S(1)}, u32[]{:S(2)}, u32[]{:S(2)}) collective-permute-start(bf16[128,768]{1,0:T(8,128)(2,1)S(1)} %fusion.55), channel_id=1, source_target_pairs={{0,16},{4,20},{8,24},{12,28},{16,0},{20,4},{24,8},{28,12},{1,17},{... | collective-permute-start | bytes 589832 | tf_op jit(solution)/shard_map/ppermute | solution.py:139
  425.4 26.1 %collective-permute-start.23 = (bf16[512,1024]{1,0:T(8,128)(2,1)S(1)}, bf16[512,1024]{1,0:T(8,128)(2,1)S(1)}, u32[]{:S(2)}, u32[]{:S(2)}) collective-permute-start(bf16[512,1024]{1,0:T(8,128)(2,1)S(1)} %fusion.21), channel_id=1, source_target_pairs={{0,2},{1,3},{2,0},{3,1},{4,6},{5,7},{6,4},{7,5},{8,10},{9,11},{10,... | collective-permute-start | bytes 3145736 | tf_op jit(solution)/shard_map/ppermute | solution.py:139
  426.0 11.9 %collective-permute-start.33 = (bf16[256,768]{1,0:T(8,128)(2,1)S(1)}, bf16[256,768]{1,0:T(8,128)(2,1)S(1)}, u32[]{:S(2)}, u32[]{:S(2)}) collective-permute-start(bf16[256,768]{1,0:T(8,128)(2,1)S(1)} %maximum_select_fusion.20), channel_id=1, source_target_pairs={{0,8},{4,12},{8,0},{12,4},{16,24},{20,28},{24,16},{28,20},{1,9},{5... | collective-permute-start | bytes 1179656 | tf_op jit(solution)/shard_map/ppermute | solution.py:139
  431.1 74.3 %collective-permute-start.17 = (bf16[512,1024]{1,0:T(8,128)(2,1)S(1)}, bf16[512,1024]{1,0:T(8,128)(2,1)S(1)}, u32[]{:S(2)}, u32[]{:S(2)}) collective-permute-start(bf16[512,1024]{1,0:T(8,128)(2,1)S(1)} %copy-done.28), channel_id=1, source_target_pairs={{0,1},{1,0},{2,3},{3,2},{4,5},{5,4},{6,7},{7,6},{8,9},{9,8},{10,11... | collective-permute-start | bytes 3145736 | tf_op jit(solution)/shard_map/ppermute | solution.py:139
  437.9 36.3 %collective-permute-start.55 = (bf16[512,1152]{1,0:T(8,128)(2,1)S(1)}, bf16[512,1152]{1,0:T(8,128)(2,1)S(1)}, u32[]{:S(2)}, u32[]{:S(2)}) collective-permute-start(bf16[512,1152]{1,0:T(8,128)(2,1)S(1)} %maximum_select_fusion.13), channel_id=1, source_target_pairs={{0,8},{4,12},{8,0},{12,4},{16,24},{20,28},{24,16},{28,20},{1,9},{5... | collective-permute-start | bytes 3538952 | tf_op jit(solution)/shard_map/ppermute | solution.py:139
  440.0 65.4 %collective-permute-start.19 = (bf16[512,1024]{1,0:T(8,128)(2,1)S(1)}, bf16[512,1024]{1,0:T(8,128)(2,1)S(1)}, u32[]{:S(2)}, u32[]{:S(2)}) collective-permute-start(bf16[512,1024]{1,0:T(8,128)(2,1)S(1)} %fusion.15), channel_id=1, source_target_pairs={{0,2},{1,3},{2,0},{3,1},{4,6},{5,7},{6,4},{7,5},{8,10},{9,11},{10,... | collective-permute-start | bytes 3145736 | tf_op jit(solution)/shard_map/ppermute | solution.py:139
  444.4 25.2 %collective-permute-start.58 = (bf16[144,1024]{1,0:T(8,128)(2,1)S(1)}, bf16[144,1024]{1,0:T(8,128)(2,1)S(1)}, u32[]{:S(2)}, u32[]{:S(2)}) collective-permute-start(bf16[144,1024]{1,0:T(8,128)(2,1)S(1)} %fusion.62), channel_id=1, source_target_pairs={{0,16},{4,20},{8,24},{12,28},{16,0},{20,4},{24,8},{28,12},{1,17},{... | collective-permute-start | bytes 884744 | tf_op jit(solution)/shard_map/ppermute | solution.py:139
  451.5 56.8 %collective-permute-start.34 = (bf16[512,768]{1,0:T(8,128)(2,1)S(1)}, bf16[512,768]{1,0:T(8,128)(2,1)S(1)}, u32[]{:S(2)}, u32[]{:S(2)}) collective-permute-start(bf16[512,768]{1,0:T(8,128)(2,1)S(1)} %maximum_select_fusion.15), channel_id=1, source_target_pairs={{0,4},{4,0},{8,12},{12,8},{16,20},{20,16},{24,28},{28,24},{1,5},{5... | collective-permute-start | bytes 2359304 | tf_op jit(solution)/shard_map/ppermute | solution.py:139
  470.8 17.0 %collective-permute-start.59 = (bf16[144,1024]{1,0:T(8,128)(2,1)S(1)}, bf16[144,1024]{1,0:T(8,128)(2,1)S(1)}, u32[]{:S(2)}, u32[]{:S(2)}) collective-permute-start(bf16[144,1024]{1,0:T(8,128)(2,1)S(1)} %fusion.50), channel_id=1, source_target_pairs={{0,16},{4,20},{8,24},{12,28},{16,0},{20,4},{24,8},{28,12},{1,17},{... | collective-permute-start | bytes 884744 | tf_op jit(solution)/shard_map/ppermute | solution.py:139
  478.6 9.5 %collective-permute-start.26 = (f32[2,1024]{1,0:T(2,128)S(1)}, f32[2,1024]{1,0:T(2,128)S(1)}, u32[]{:S(2)}, u32[]{:S(2)}) collective-permute-start(f32[2,1024]{1,0:T(2,128)S(1)} %fusion.98), channel_id=1, source_target_pairs={{0,4},{4,0},{8,12},{12,8},{16,20},{20,16},{24,28},{28,24},{1,5},{5... | collective-permute-start | bytes 24584 | tf_op jit(solution)/shard_map/ppermute | solution.py:139
  488.0 15.2 %collective-permute-start.60 = (bf16[288,1024]{1,0:T(8,128)(2,1)S(1)}, bf16[288,1024]{1,0:T(8,128)(2,1)S(1)}, u32[]{:S(2)}, u32[]{:S(2)}) collective-permute-start(bf16[288,1024]{1,0:T(8,128)(2,1)S(1)} %maximum_select_fusion.18), channel_id=1, source_target_pairs={{0,8},{4,12},{8,0},{12,4},{16,24},{20,28},{24,16},{28,20},{1,9},{5... | collective-permute-start | bytes 1769480 | tf_op jit(solution)/shard_map/ppermute | solution.py:139
  488.1 15.0 %collective-permute-start.27 = (f32[2,1024]{1,0:T(2,128)S(1)}, f32[2,1024]{1,0:T(2,128)S(1)}, u32[]{:S(2)}, u32[]{:S(2)}) collective-permute-start(f32[2,1024]{1,0:T(2,128)S(1)} %add.333), channel_id=1, source_target_pairs={{0,8},{4,12},{8,0},{12,4},{16,24},{20,28},{24,16},{28,20},{1,9},{5... | collective-permute-start | bytes 24584 | tf_op jit(solution)/shard_map/ppermute | solution.py:139
  503.7 26.7 %collective-permute-start.61 = (bf16[576,1024]{1,0:T(8,128)(2,1)S(1)}, bf16[576,1024]{1,0:T(8,128)(2,1)S(1)}, u32[]{:S(2)}, u32[]{:S(2)}) collective-permute-start(bf16[576,1024]{1,0:T(8,128)(2,1)S(1)} %maximum_select_fusion.14), channel_id=1, source_target_pairs={{0,4},{4,0},{8,12},{12,8},{16,20},{20,16},{24,28},{28,24},{1,5},{5... | collective-permute-start | bytes 3538952 | tf_op jit(solution)/shard_map/ppermute | solution.py:139
  (54 other events, 450.4 us)
